TPU v7x, 32 devices: a whole 2x2x4 slice. The times are simulated.
32 devices in a mesh: groups: 2 (over y), ctx: 8 (over z, x), head: 2 (over core).
Axes of the slice: x: 2, y: 2, z: 4, core: 2. Of those that a mesh axis runs over, the one named last changes fastest.
Arguments:
- queries: bfloat16 [4096, 512], P(('groups', 'ctx'), 'head'), parts along dimension 0, may hold values from -5 to 5
- key_input: bfloat16 [4096, 128], P(('groups', 'ctx')), parts along dimension 0, may hold values from -5 to 5
- value_input: bfloat16 [4096, 128], P(('groups', 'ctx')), parts along dimension 0, may hold values from -2.5 to 2.5
- grad_out: bfloat16 [4096, 512], P(('groups', 'ctx'), 'head'), parts along dimension 0, may hold values from -1.5 to 1.5
- doc_lengths: int32 [32], P('groups'), parts along dimension 0, may hold values from 1 to 512, 2048 in all
- stretch_plan: int32 [32], P(('groups', 'ctx')), parts along dimension 0, may hold values from 0 to 15, as said below
Outputs:
- output: bfloat16 [4096, 512], P(('groups', 'ctx'), 'head'), parts along dimension 0
- query_grad: float32 [4096, 512], P(('groups', 'ctx'), 'head'), parts along dimension 0
- key_grad: float32 [4096, 128], P(('groups', 'ctx')), parts along dimension 0
- value_grad: float32 [4096, 128], P(('groups', 'ctx')), parts along dimension 0
There are 2 independent parts, one for each index of `groups`. A program takes and returns all parts, laid end to end along the dimension named above; each array names one. Nothing has to cross between parts.
Inputs may be any that keep to these rules, and one draw needn't show every extreme that they name: A permutation of the stretch numbers: slot j holds stretch stretch_plan[j], and |stretch_plan[j] - j| <= 4 for every slot, with equality for some slot.
All inputs are finite; a program needn't handle non-finite values.
Results may differ from a plain program's by a relative error of at most 0.025.
Values may be sent and summed in bfloat16 or wider, within the bound.
A program may use at most 64 MiB of HBM per device.

v0:
```python
import math

import jax
import jax.numpy as jnp
from jax import lax
from jax.sharding import PartitionSpec as P

HOPS = 2
DOC_CAP = 4096


neg_large = -1e30


def shortened(value):
    return jax.tree.map(lambda a: a.astype(jnp.bfloat16) if a.dtype == jnp.float32 else a, value)


def from_behind(block, axis, distance):
    devices = range(lax.axis_size(axis))
    route = [((i - distance) % len(devices), i) for i in devices]
    return lax.ppermute(block, axis, route)


def shifted(value, axis, by):
    count = lax.axis_size(axis)
    pairs = [(i, i + by) for i in range(count) if 0 <= i + by < count]
    return lax.ppermute(value, axis, pairs)


def doc_numbers(bounds, places):
    return jnp.sum((bounds[None, :] <= places[:, None]).astype(jnp.int32), axis=1)


def per_device(queries, key_input, value_input, grad_out, doc_lengths, stretch_plan):
    tok_dev = key_input.shape[0]
    head_dim = key_input.shape[1]
    heads_here = queries.shape[1] // head_dim
    query_width = heads_here * head_dim
    stretch_rows = tok_dev // 2
    ctx_size = lax.axis_size("ctx")
    device_index = lax.axis_index("ctx")
    doc_max = min(DOC_CAP, tok_dev * ctx_size // 4)
    reach_blocks = doc_max // tok_dev
    visits = reach_blocks + 2 * HOPS + 1
    inv_root = 1.0 / math.sqrt(head_dim)
    bounds = jnp.cumsum(doc_lengths)

    def shift_blocks(block_pair, hops):
        return jax.tree.map(
            lambda part, own: part.astype(own.dtype),
            from_behind(shortened(block_pair), "ctx", hops),
            block_pair,
        )

    def shift_grads(grad_pair, hops):
        return from_behind(grad_pair, "ctx", hops)

    def first_blocks():
        return (key_input, value_input)

    def add_grads(moving, key_term, value_term):
        return (moving[0] + key_term, moving[1] + value_term)

    both_rows = jnp.concatenate([queries, grad_out], axis=1)
    pieces = []
    for offset in range(-HOPS, HOPS + 1):
        if offset == 0:
            pieces.append(both_rows)
        else:
            pieces.append(shifted(both_rows, "ctx", -offset))
    window = jnp.concatenate(pieces, axis=0)
    first_row = (device_index - HOPS) * tok_dev
    slot_rows = [
        lax.dynamic_slice_in_dim(
            window, stretch_plan[slot_index] * stretch_rows - first_row, stretch_rows, 0
        )
        for slot_index in range(2)
    ]
    local_rows = jnp.concatenate(slot_rows, axis=0)
    query_heads = local_rows[:, :query_width].reshape(tok_dev, heads_here, head_dim)
    grad_heads = local_rows[:, query_width:].reshape(tok_dev, heads_here, head_dim)
    stretch_offsets = jnp.arange(stretch_rows, dtype=jnp.int32)
    query_places = jnp.concatenate(
        [
            stretch_plan[0] * stretch_rows + stretch_offsets,
            stretch_plan[1] * stretch_rows + stretch_offsets,
        ]
    )
    query_docs = doc_numbers(bounds, query_places)
    key_offsets = jnp.arange(tok_dev, dtype=jnp.int32)

    def block_mask(source):
        key_places = source * tok_dev + key_offsets
        key_docs = doc_numbers(bounds, key_places)
        inside = (source >= 0) & (source < ctx_size)
        same_doc = (query_docs[:, None] == key_docs[None, :]) & (
            key_places[None, :] <= query_places[:, None]
        )
        return same_doc & inside

    def masked_scores(block_keys, allowed):
        products = (
            jnp.einsum("phd,td->pht", query_heads, block_keys, preferred_element_type=jnp.float32)
            * inv_root
        )
        return jnp.where(allowed[:, None, :], products, neg_large)

    def stats_terms(stats, block_pair, source):
        allowed = block_mask(source)
        row_top, row_total = stats
        scores = masked_scores(block_pair[0], allowed)
        new_top = jnp.maximum(row_top, jnp.max(scores, axis=2))
        exps = jnp.where(allowed[:, None, :], jnp.exp(scores - new_top[:, :, None]), 0.0)
        row_total = row_total * jnp.exp(row_top - new_top) + jnp.sum(exps, axis=2)
        return (new_top, row_total)

    stats = (
        jnp.full((tok_dev, heads_here), neg_large, jnp.float32),
        jnp.zeros((tok_dev, heads_here), jnp.float32),
    )

    def stats_step(carried, step_number):
        block_pair, stats = carried
        stats = stats_terms(stats, block_pair, device_index + HOPS - step_number)
        stored = None
        return ((shift_blocks(block_pair, 1), stats), stored)

    steps_all = jnp.arange(visits - 1, dtype=jnp.int32)
    start_block = shift_blocks(first_blocks(), -HOPS)
    (last_block, stats), stored = lax.scan(stats_step, (start_block, stats), steps_all)
    stats = stats_terms(stats, last_block, device_index + HOPS - (visits - 1))
    row_top, row_total = stats
    log_total = row_top + jnp.log(row_total)

    def value_terms(weighted, block_pair, source):
        allowed = block_mask(source)
        scores = masked_scores(block_pair[0], allowed)
        weights = jnp.where(allowed[:, None, :], jnp.exp(scores - log_total[:, :, None]), 0.0)
        return weighted + jnp.einsum(
            "pht,td->phd",
            weights.astype(jnp.bfloat16),
            block_pair[1],
            preferred_element_type=jnp.float32,
        )

    weighted = jnp.zeros((tok_dev, heads_here, head_dim), jnp.float32)

    def weighted_step(carried, step_number):
        block_pair, total = carried
        total = value_terms(total, block_pair, device_index + HOPS - step_number)
        return ((shift_blocks(block_pair, 1), total), None)

    second_block = shift_blocks(first_blocks(), -HOPS)
    (second_last, weighted), unused = lax.scan(weighted_step, (second_block, weighted), steps_all)
    weighted = value_terms(weighted, second_last, device_index + HOPS - (visits - 1))
    attended = weighted.astype(jnp.bfloat16)
    row_dots = jnp.sum(grad_heads.astype(jnp.float32) * attended.astype(jnp.float32), axis=2)

    def backward_terms(query_acc, block_pair, source):
        allowed = block_mask(source)
        backward_query_acc = query_acc
        scores = masked_scores(block_pair[0], allowed)
        weights = jnp.where(allowed[:, None, :], jnp.exp(scores - log_total[:, :, None]), 0.0)
        value_acc = jnp.einsum(
            "pht,phd->td",
            weights.astype(jnp.bfloat16),
            grad_heads,
            preferred_element_type=jnp.float32,
        )
        grad_weights = jnp.einsum(
            "phd,td->pht", grad_heads, block_pair[1], preferred_element_type=jnp.float32
        )
        grad_scores = (weights * (grad_weights - row_dots[:, :, None])).astype(jnp.bfloat16)
        backward_query_acc = backward_query_acc + jnp.einsum(
            "pht,td->phd", grad_scores, block_pair[0], preferred_element_type=jnp.float32
        )
        key_acc = jnp.einsum(
            "pht,phd->td", grad_scores, query_heads, preferred_element_type=jnp.float32
        )
        return (backward_query_acc, key_acc, value_acc)

    query_acc = jnp.zeros((tok_dev, heads_here, head_dim), jnp.float32)
    moving = (
        jnp.zeros((tok_dev, head_dim), jnp.float32),
        jnp.zeros((tok_dev, head_dim), jnp.float32),
    )

    def backward_step(carried, step_number):
        block_pair, query_acc, moving = carried
        query_acc, key_term, value_term = backward_terms(
            query_acc, block_pair, device_index + HOPS - step_number
        )
        moving = add_grads(moving, key_term, value_term)
        return ((shift_blocks(block_pair, 1), query_acc, shift_grads(moving, 1)), None)

    again_block = shift_blocks(first_blocks(), -HOPS)
    (final_block, query_acc, moving), unused = lax.scan(
        backward_step, (again_block, query_acc, moving), steps_all
    )
    query_acc, key_term, value_term = backward_terms(
        query_acc, final_block, device_index + HOPS - (visits - 1)
    )
    moving = add_grads(moving, key_term, value_term)
    moving = shift_grads(moving, -(reach_blocks + HOPS))
    key_sum, value_sum = lax.psum(moving, "head")
    output = attended.reshape(tok_dev, query_width)
    query_grad = (query_acc * inv_root).reshape(tok_dev, query_width)
    key_grad = key_sum * inv_root
    return (output, query_grad, key_grad, value_sum)


def solution(mesh):
    return jax.shard_map(
        per_device,
        mesh=mesh,
        in_specs=(
            P(("groups", "ctx"), "head"),
            P(("groups", "ctx"), None),
            P(("groups", "ctx"), None),
            P(("groups", "ctx"), "head"),
            P("groups"),
            P(("groups", "ctx")),
        ),
        out_specs=(
            P(("groups", "ctx"), "head"),
            P(("groups", "ctx"), "head"),
            P(("groups", "ctx"), None),
            P(("groups", "ctx"), None),
        ),
        check_vma=False,
    )
```

profile of v0, /device:TPU:0, one launch (start us, length us, event | category | flops | bytes accessed | tf_op | source)
XLA Modules:
  0.0 252.6 jit_solution(7476120381572225535)
XLA Ops:
  9.3 4.9 %collective-permute-start.9 = (bf16[256,512]{0,1:T(8,128)(2,1)S(1)}, bf16[256,512]{0,1:T(8,128)(2,1)S(1)}, u32[]{:S(2)}, u32[]{:S(2)}) collective-permute-start(bf16[256,512]{0,1:T(8,128)(2,1)S(1)} %pad_maximum_fusion), channel_id=1, source_target_pairs={{0,4},{2,6},{4,8},{6,10},{8,12},{10,14},{1,5},{3,7},{5,9},{7,11},{... | collective-permute-start | bytes 786440 | tf_op jit(solution)/shard_map/ppermute | solution.py:28
  14.2 3.4 %collective-permute-start.10 = (bf16[256,512]{0,1:T(8,128)(2,1)S(1)}, bf16[256,512]{0,1:T(8,128)(2,1)S(1)}, u32[]{:S(2)}, u32[]{:S(2)}) collective-permute-start(bf16[256,512]{0,1:T(8,128)(2,1)S(1)} %pad_maximum_fusion), channel_id=1, source_target_pairs={{0,2},{2,4},{4,6},{6,8},{8,10},{10,12},{12,14},{1,3},{3,5},{5,7},{... | collective-permute-start | bytes 786440 | tf_op jit(solution)/shard_map/ppermute | solution.py:28
  28.3 6.1 %collective-permute-done.11 = bf16[256,512]{0,1:T(8,128)(2,1)S(1)} collective-permute-done((bf16[256,512]{0,1:T(8,128)(2,1)S(1)}, bf16[256,512]{0,1:T(8,128)(2,1)S(1)}, u32[]{:S(2)}, u32[]{:S(2)}) %collective-permute-start.11) | collective-permute-done | bytes 262176 | tf_op jit(solution)/shard_map/ppermute | solution.py:28
  34.4 5.3 %collective-permute-done.12 = bf16[256,512]{0,1:T(8,128)(2,1)S(1)} collective-permute-done((bf16[256,512]{0,1:T(8,128)(2,1)S(1)}, bf16[256,512]{0,1:T(8,128)(2,1)S(1)}, u32[]{:S(2)}, u32[]{:S(2)}) %collective-permute-start.12) | collective-permute-done | bytes 262176 | tf_op jit(solution)/shard_map/ppermute | solution.py:28
  39.9 42.1 %while.55 = (s32[]{:T(128)}, bf16[256,128]{1,0:T(8,128)(2,1)S(1)}, f32[256,2]{0,1:T(2,128)S(1)}, f32[256,2]{0,1:T(2,128)S(1)}, s32[256]{0:T(256)S(1)}, /*index=5...) while((s32[]{:T(128)}, bf16[256,128]{1,0:T(8,128)(2,1)S(1)}, ...), condition=%wide.region_6.7_spmd.clone, body=%wide.region_2.6_spmd.clone.sunk | while | flops 34617864 | bytes 1869110 | solution.py:131
  42.1 4.9 %collective-permute-done = bf16[256,128]{1,0:T(8,128)(2,1)S(1)} collective-permute-done((bf16[256,128]{1,0:T(8,128)(2,1)S(1)}, bf16[256,128]{1,0:T(8,128)(2,1)S(1)}, u32[]{:S(2)}, u32[]{:S(2)}) %collective-permute-start) | collective-permute-done | bytes 65568 | tf_op jit(solution)/shard_map/while/body/eval_jaxpr/ppermute | solution.py:22
  49.1 4.9 %collective-permute-done = bf16[256,128]{1,0:T(8,128)(2,1)S(1)} collective-permute-done((bf16[256,128]{1,0:T(8,128)(2,1)S(1)}, bf16[256,128]{1,0:T(8,128)(2,1)S(1)}, u32[]{:S(2)}, u32[]{:S(2)}) %collective-permute-start) | collective-permute-done | bytes 65568 | tf_op jit(solution)/shard_map/while/body/eval_jaxpr/ppermute | solution.py:22
  56.0 5.0 %collective-permute-done = bf16[256,128]{1,0:T(8,128)(2,1)S(1)} collective-permute-done((bf16[256,128]{1,0:T(8,128)(2,1)S(1)}, bf16[256,128]{1,0:T(8,128)(2,1)S(1)}, u32[]{:S(2)}, u32[]{:S(2)}) %collective-permute-start) | collective-permute-done | bytes 65568 | tf_op jit(solution)/shard_map/while/body/eval_jaxpr/ppermute | solution.py:22
  63.1 5.0 %collective-permute-done = bf16[256,128]{1,0:T(8,128)(2,1)S(1)} collective-permute-done((bf16[256,128]{1,0:T(8,128)(2,1)S(1)}, bf16[256,128]{1,0:T(8,128)(2,1)S(1)}, u32[]{:S(2)}, u32[]{:S(2)}) %collective-permute-start) | collective-permute-done | bytes 65568 | tf_op jit(solution)/shard_map/while/body/eval_jaxpr/ppermute | solution.py:22
  70.2 4.9 %collective-permute-done = bf16[256,128]{1,0:T(8,128)(2,1)S(1)} collective-permute-done((bf16[256,128]{1,0:T(8,128)(2,1)S(1)}, bf16[256,128]{1,0:T(8,128)(2,1)S(1)}, u32[]{:S(2)}, u32[]{:S(2)}) %collective-permute-start) | collective-permute-done | bytes 65568 | tf_op jit(solution)/shard_map/while/body/eval_jaxpr/ppermute | solution.py:22
  77.2 4.9 %collective-permute-done = bf16[256,128]{1,0:T(8,128)(2,1)S(1)} collective-permute-done((bf16[256,128]{1,0:T(8,128)(2,1)S(1)}, bf16[256,128]{1,0:T(8,128)(2,1)S(1)}, u32[]{:S(2)}, u32[]{:S(2)}) %collective-permute-start) | collective-permute-done | bytes 65568 | tf_op jit(solution)/shard_map/while/body/eval_jaxpr/ppermute | solution.py:22
  82.5 48.9 %while.56 = (s32[]{:T(128)}, bf16[256,128]{1,0:T(8,128)(2,1)S(1)}, bf16[256,128]{1,0:T(8,128)(2,1)S(1)}, f32[256,2,128]{2,0,1:T(8,128)S(1)}, s32[256]{0:T(256)S(...) while((s32[]{:T(128)}, bf16[256,128]{1,0:T(8,128)(2,1)S(1)}, ...), condition=%wide.region_12.13_spmd.clone, body=%wide.region_10.12_spmd.clone.sunk | while | flops 68169736 | bytes 1713509 | solution.py:155
  84.6 4.9 %collective-permute-done.1 = bf16[256,128]{1,0:T(8,128)(2,1)S(1)} collective-permute-done((bf16[256,128]{1,0:T(8,128)(2,1)S(1)}, bf16[256,128]{1,0:T(8,128)(2,1)S(1)}, u32[]{:S(2)}, u32[]{:S(2)}) %collective-permute-start.1) | collective-permute-done | bytes 65568 | tf_op jit(solution)/shard_map/while/body/eval_jaxpr/ppermute | solution.py:22
  92.3 4.9 %collective-permute-done.1 = bf16[256,128]{1,0:T(8,128)(2,1)S(1)} collective-permute-done((bf16[256,128]{1,0:T(8,128)(2,1)S(1)}, bf16[256,128]{1,0:T(8,128)(2,1)S(1)}, u32[]{:S(2)}, u32[]{:S(2)}) %collective-permute-start.1) | collective-permute-done | bytes 65568 | tf_op jit(solution)/shard_map/while/body/eval_jaxpr/ppermute | solution.py:22
  100.0 4.9 %collective-permute-done.1 = bf16[256,128]{1,0:T(8,128)(2,1)S(1)} collective-permute-done((bf16[256,128]{1,0:T(8,128)(2,1)S(1)}, bf16[256,128]{1,0:T(8,128)(2,1)S(1)}, u32[]{:S(2)}, u32[]{:S(2)}) %collective-permute-start.1) | collective-permute-done | bytes 65568 | tf_op jit(solution)/shard_map/while/body/eval_jaxpr/ppermute | solution.py:22
  107.8 5.5 %collective-permute-done.1 = bf16[256,128]{1,0:T(8,128)(2,1)S(1)} collective-permute-done((bf16[256,128]{1,0:T(8,128)(2,1)S(1)}, bf16[256,128]{1,0:T(8,128)(2,1)S(1)}, u32[]{:S(2)}, u32[]{:S(2)}) %collective-permute-start.1) | collective-permute-done | bytes 65568 | tf_op jit(solution)/shard_map/while/body/eval_jaxpr/ppermute | solution.py:22
  116.8 5.6 %collective-permute-done.1 = bf16[256,128]{1,0:T(8,128)(2,1)S(1)} collective-permute-done((bf16[256,128]{1,0:T(8,128)(2,1)S(1)}, bf16[256,128]{1,0:T(8,128)(2,1)S(1)}, u32[]{:S(2)}, u32[]{:S(2)}) %collective-permute-start.1) | collective-permute-done | bytes 65568 | tf_op jit(solution)/shard_map/while/body/eval_jaxpr/ppermute | solution.py:22
  125.8 4.9 %collective-permute-done.1 = bf16[256,128]{1,0:T(8,128)(2,1)S(1)} collective-permute-done((bf16[256,128]{1,0:T(8,128)(2,1)S(1)}, bf16[256,128]{1,0:T(8,128)(2,1)S(1)}, u32[]{:S(2)}, u32[]{:S(2)}) %collective-permute-start.1) | collective-permute-done | bytes 65568 | tf_op jit(solution)/shard_map/while/body/eval_jaxpr/ppermute | solution.py:22
  132.2 82.6 %while.57 = (s32[]{:T(128)}, bf16[256,128]{1,0:T(8,128)(2,1)S(1)}, bf16[256,128]{1,0:T(8,128)(2,1)S(1)}, f32[256,2,128]{2,0,1:T(8,128)S(1)}, f32[256,128]{1,0:T(...) while((s32[]{:T(128)}, bf16[256,128]{1,0:T(8,128)(2,1)S(1)}, ...), condition=%wide.region_16.17_spmd.clone, body=%wide.region_14.16_spmd.clone.sunk | while | flops 169291776 | bytes 6106581 | solution.py:198
  135.4 3.9 %collective-permute-done.3 = bf16[256,128]{1,0:T(8,128)(2,1)S(1)} collective-permute-done((bf16[256,128]{1,0:T(8,128)(2,1)S(1)}, bf16[256,128]{1,0:T(8,128)(2,1)S(1)}, u32[]{:S(2)}, u32[]{:S(2)}) %collective-permute-start.3) | collective-permute-done | bytes 65568 | tf_op jit(solution)/shard_map/while/body/eval_jaxpr/ppermute | solution.py:22
  148.5 3.4 %collective-permute-start.6 = (f32[256,128]{1,0:T(8,128)S(1)}, f32[256,128]{1,0:T(8,128)S(1)}, u32[]{:S(2)}, u32[]{:S(2)}) collective-permute-start(f32[256,128]{1,0:T(8,128)S(1)} %fusion.133), channel_id=1, source_target_pairs={{14,0},{0,2},{2,4},{4,6},{6,8},{8,10},{10,12},{12,14},{15,1},{1,3}... | collective-permute-start | bytes 393224 | tf_op jit(solution)/shard_map/while/body/eval_jaxpr/ppermute | solution.py:22
  183.1 4.4 %collective-permute-done.5 = f32[256,128]{1,0:T(8,128)S(1)} collective-permute-done((f32[256,128]{1,0:T(8,128)S(1)}, f32[256,128]{1,0:T(8,128)S(1)}, u32[]{:S(2)}, u32[]{:S(2)}) %collective-permute-start.5) | collective-permute-done | bytes 131104 | tf_op jit(solution)/shard_map/while/body/eval_jaxpr/ppermute | solution.py:22
  218.9 4.4 %collective-permute-done.14 = f32[256,128]{1,0:T(8,128)S(1)} collective-permute-done((f32[256,128]{1,0:T(8,128)S(1)}, f32[256,128]{1,0:T(8,128)S(1)}, u32[]{:S(2)}, u32[]{:S(2)}) %collective-permute-start.14) | collective-permute-done | bytes 131104 | tf_op jit(solution)/shard_map/ppermute | solution.py:22
  227.4 15.2 %all-reduce.3.cloned.1.call-done = (f32[256,128]{1,0:T(8,128)}, f32[256,128]{1,0:T(8,128)}) async-done(((f32[256,128]{1,0:T(8,128)}, f32[256,128]{1,0:T(8,128)}), (f32[256,128]{1,0:T(8,128)}, f32[256,128]{1,0:T(8,128)})) %all-reduce.3.cloned.1.call-update) | async-done | bytes 262160 | tf_op jit(solution)/shard_map/psum | solution.py:206
  (307 shorter events, 111.9 us)
Async XLA Ops:
  7.2 235.4 %all-reduce.3.cloned.1.call-start = ((), (), s32[]{:S(2)}) async-start(), calls=%async_computation | async-start | bytes 524288 | tf_op jit(solution)/shard_map/psum | solution.py:206
  9.3 19.0 %collective-permute-start.9 = (bf16[256,512]{0,1:T(8,128)(2,1)S(1)}, bf16[256,512]{0,1:T(8,128)(2,1)S(1)}, u32[]{:S(2)}, u32[]{:S(2)}) collective-permute-start(bf16[256,512]{0,1:T(8,128)(2,1)S(1)} %pad_maximum_fusion), channel_id=1, source_target_pairs={{0,4},{2,6},{4,8},{6,10},{8,12},{10,14},{1,5},{3,7},{5,9},{7,11},{... | collective-permute-start | bytes 786440 | tf_op jit(solution)/shard_map/ppermute | solution.py:28
  14.2 14.1 %collective-permute-start.10 = (bf16[256,512]{0,1:T(8,128)(2,1)S(1)}, bf16[256,512]{0,1:T(8,128)(2,1)S(1)}, u32[]{:S(2)}, u32[]{:S(2)}) collective-permute-start(bf16[256,512]{0,1:T(8,128)(2,1)S(1)} %pad_maximum_fusion), channel_id=1, source_target_pairs={{0,2},{2,4},{4,6},{6,8},{8,10},{10,12},{12,14},{1,3},{3,5},{5,7},{... | collective-permute-start | bytes 786440 | tf_op jit(solution)/shard_map/ppermute | solution.py:28
  17.6 9.2 %collective-permute-start.7 = (bf16[256,128]{1,0:T(8,128)(2,1)}, bf16[256,128]{1,0:T(8,128)(2,1)S(1)}, u32[]{:S(2)}, u32[]{:S(2)}) collective-permute-start(bf16[256,128]{1,0:T(8,128)(2,1)} %param.13), channel_id=1, source_target_pairs={{4,0},{6,2},{8,4},{10,6},{12,8},{14,10},{0,12},{2,14},{5,1},{7,3},... | collective-permute-start | bytes 196616 | tf_op jit(solution)/shard_map/ppermute | solution.py:22
  19.1 9.1 %collective-permute-start.8 = (bf16[256,128]{1,0:T(8,128)(2,1)}, bf16[256,128]{1,0:T(8,128)(2,1)S(1)}, u32[]{:S(2)}, u32[]{:S(2)}) collective-permute-start(bf16[256,128]{1,0:T(8,128)(2,1)} %param.14), channel_id=1, source_target_pairs={{4,0},{6,2},{8,4},{10,6},{12,8},{14,10},{0,12},{2,14},{5,1},{7,3},... | collective-permute-start | bytes 196616 | tf_op jit(solution)/shard_map/ppermute | solution.py:22
  25.6 8.8 %collective-permute-start.11 = (bf16[256,512]{0,1:T(8,128)(2,1)S(1)}, bf16[256,512]{0,1:T(8,128)(2,1)S(1)}, u32[]{:S(2)}, u32[]{:S(2)}) collective-permute-start(bf16[256,512]{0,1:T(8,128)(2,1)S(1)} %pad_maximum_fusion), channel_id=1, source_target_pairs={{2,0},{4,2},{6,4},{8,6},{10,8},{12,10},{14,12},{3,1},{5,3},{7,5},{... | collective-permute-start | bytes 786440 | tf_op jit(solution)/shard_map/ppermute | solution.py:28
  26.9 12.8 %collective-permute-start.12 = (bf16[256,512]{0,1:T(8,128)(2,1)S(1)}, bf16[256,512]{0,1:T(8,128)(2,1)S(1)}, u32[]{:S(2)}, u32[]{:S(2)}) collective-permute-start(bf16[256,512]{0,1:T(8,128)(2,1)S(1)} %pad_maximum_fusion), channel_id=1, source_target_pairs={{4,0},{6,2},{8,4},{10,6},{12,8},{14,10},{5,1},{7,3},{9,5},{11,7},{... | collective-permute-start | bytes 786440 | tf_op jit(solution)/shard_map/ppermute | solution.py:28
  97.9 7.8 %collective-permute-start.2 = (bf16[256,128]{1,0:T(8,128)(2,1)S(1)}, bf16[256,128]{1,0:T(8,128)(2,1)S(1)}, u32[]{:S(2)}, u32[]{:S(2)}) collective-permute-start(bf16[256,128]{1,0:T(8,128)(2,1)S(1)} %copy.117), channel_id=1, source_target_pairs={{14,0},{0,2},{2,4},{4,6},{6,8},{8,10},{10,12},{12,14},{15,1},{1,3}... | collective-permute-start | bytes 196616 | tf_op jit(solution)/shard_map/while/body/eval_jaxpr/ppermute | solution.py:22
  105.8 8.9 %collective-permute-start.2 = (bf16[256,128]{1,0:T(8,128)(2,1)S(1)}, bf16[256,128]{1,0:T(8,128)(2,1)S(1)}, u32[]{:S(2)}, u32[]{:S(2)}) collective-permute-start(bf16[256,128]{1,0:T(8,128)(2,1)S(1)} %copy.117), channel_id=1, source_target_pairs={{14,0},{0,2},{2,4},{4,6},{6,8},{8,10},{10,12},{12,14},{15,1},{1,3}... | collective-permute-start | bytes 196616 | tf_op jit(solution)/shard_map/while/body/eval_jaxpr/ppermute | solution.py:22
  114.7 9.0 %collective-permute-start.2 = (bf16[256,128]{1,0:T(8,128)(2,1)S(1)}, bf16[256,128]{1,0:T(8,128)(2,1)S(1)}, u32[]{:S(2)}, u32[]{:S(2)}) collective-permute-start(bf16[256,128]{1,0:T(8,128)(2,1)S(1)} %copy.117), channel_id=1, source_target_pairs={{14,0},{0,2},{2,4},{4,6},{6,8},{8,10},{10,12},{12,14},{15,1},{1,3}... | collective-permute-start | bytes 196616 | tf_op jit(solution)/shard_map/while/body/eval_jaxpr/ppermute | solution.py:22
  134.7 8.1 %collective-permute-start.5 = (f32[256,128]{1,0:T(8,128)S(1)}, f32[256,128]{1,0:T(8,128)S(1)}, u32[]{:S(2)}, u32[]{:S(2)}) collective-permute-start(f32[256,128]{1,0:T(8,128)S(1)} %fusion.132), channel_id=1, source_target_pairs={{14,0},{0,2},{2,4},{4,6},{6,8},{8,10},{10,12},{12,14},{15,1},{1,3}... | collective-permute-start | bytes 393224 | tf_op jit(solution)/shard_map/while/body/eval_jaxpr/ppermute | solution.py:22
  135.1 10.2 %collective-permute-start.6 = (f32[256,128]{1,0:T(8,128)S(1)}, f32[256,128]{1,0:T(8,128)S(1)}, u32[]{:S(2)}, u32[]{:S(2)}) collective-permute-start(f32[256,128]{1,0:T(8,128)S(1)} %fusion.133), channel_id=1, source_target_pairs={{14,0},{0,2},{2,4},{4,6},{6,8},{8,10},{10,12},{12,14},{15,1},{1,3}... | collective-permute-start | bytes 393224 | tf_op jit(solution)/shard_map/while/body/eval_jaxpr/ppermute | solution.py:22
  148.5 9.2 %collective-permute-start.6 = (f32[256,128]{1,0:T(8,128)S(1)}, f32[256,128]{1,0:T(8,128)S(1)}, u32[]{:S(2)}, u32[]{:S(2)}) collective-permute-start(f32[256,128]{1,0:T(8,128)S(1)} %fusion.133), channel_id=1, source_target_pairs={{14,0},{0,2},{2,4},{4,6},{6,8},{8,10},{10,12},{12,14},{15,1},{1,3}... | collective-permute-start | bytes 393224 | tf_op jit(solution)/shard_map/while/body/eval_jaxpr/ppermute | solution.py:22
  157.7 11.7 %collective-permute-start.3 = (bf16[256,128]{1,0:T(8,128)(2,1)S(1)}, bf16[256,128]{1,0:T(8,128)(2,1)S(1)}, u32[]{:S(2)}, u32[]{:S(2)}) collective-permute-start(bf16[256,128]{1,0:T(8,128)(2,1)S(1)} %copy.130), channel_id=1, source_target_pairs={{14,0},{0,2},{2,4},{4,6},{6,8},{8,10},{10,12},{12,14},{15,1},{1,3}... | collective-permute-start | bytes 196616 | tf_op jit(solution)/shard_map/while/body/eval_jaxpr/ppermute | solution.py:22
  157.7 11.6 %collective-permute-start.4 = (bf16[256,128]{1,0:T(8,128)(2,1)S(1)}, bf16[256,128]{1,0:T(8,128)(2,1)S(1)}, u32[]{:S(2)}, u32[]{:S(2)}) collective-permute-start(bf16[256,128]{1,0:T(8,128)(2,1)S(1)} %copy.131), channel_id=1, source_target_pairs={{14,0},{0,2},{2,4},{4,6},{6,8},{8,10},{10,12},{12,14},{15,1},{1,3}... | collective-permute-start | bytes 196616 | tf_op jit(solution)/shard_map/while/body/eval_jaxpr/ppermute | solution.py:22
  163.1 8.6 %collective-permute-start.5 = (f32[256,128]{1,0:T(8,128)S(1)}, f32[256,128]{1,0:T(8,128)S(1)}, u32[]{:S(2)}, u32[]{:S(2)}) collective-permute-start(f32[256,128]{1,0:T(8,128)S(1)} %fusion.132), channel_id=1, source_target_pairs={{14,0},{0,2},{2,4},{4,6},{6,8},{8,10},{10,12},{12,14},{15,1},{1,3}... | collective-permute-start | bytes 393224 | tf_op jit(solution)/shard_map/while/body/eval_jaxpr/ppermute | solution.py:22
  165.9 9.1 %collective-permute-start.6 = (f32[256,128]{1,0:T(8,128)S(1)}, f32[256,128]{1,0:T(8,128)S(1)}, u32[]{:S(2)}, u32[]{:S(2)}) collective-permute-start(f32[256,128]{1,0:T(8,128)S(1)} %fusion.133), channel_id=1, source_target_pairs={{14,0},{0,2},{2,4},{4,6},{6,8},{8,10},{10,12},{12,14},{15,1},{1,3}... | collective-permute-start | bytes 393224 | tf_op jit(solution)/shard_map/while/body/eval_jaxpr/ppermute | solution.py:22
  175.0 8.1 %collective-permute-start.4 = (bf16[256,128]{1,0:T(8,128)(2,1)S(1)}, bf16[256,128]{1,0:T(8,128)(2,1)S(1)}, u32[]{:S(2)}, u32[]{:S(2)}) collective-permute-start(bf16[256,128]{1,0:T(8,128)(2,1)S(1)} %copy.131), channel_id=1, source_target_pairs={{14,0},{0,2},{2,4},{4,6},{6,8},{8,10},{10,12},{12,14},{15,1},{1,3}... | collective-permute-start | bytes 196616 | tf_op jit(solution)/shard_map/while/body/eval_jaxpr/ppermute | solution.py:22
  180.2 8.7 %collective-permute-start.6 = (f32[256,128]{1,0:T(8,128)S(1)}, f32[256,128]{1,0:T(8,128)S(1)}, u32[]{:S(2)}, u32[]{:S(2)}) collective-permute-start(f32[256,128]{1,0:T(8,128)S(1)} %fusion.133), channel_id=1, source_target_pairs={{14,0},{0,2},{2,4},{4,6},{6,8},{8,10},{10,12},{12,14},{15,1},{1,3}... | collective-permute-start | bytes 393224 | tf_op jit(solution)/shard_map/while/body/eval_jaxpr/ppermute | solution.py:22
  192.4 8.7 %collective-permute-start.6 = (f32[256,128]{1,0:T(8,128)S(1)}, f32[256,128]{1,0:T(8,128)S(1)}, u32[]{:S(2)}, u32[]{:S(2)}) collective-permute-start(f32[256,128]{1,0:T(8,128)S(1)} %fusion.133), channel_id=1, source_target_pairs={{14,0},{0,2},{2,4},{4,6},{6,8},{8,10},{10,12},{12,14},{15,1},{1,3}... | collective-permute-start | bytes 393224 | tf_op jit(solution)/shard_map/while/body/eval_jaxpr/ppermute | solution.py:22
  201.1 8.2 %collective-permute-start.3 = (bf16[256,128]{1,0:T(8,128)(2,1)S(1)}, bf16[256,128]{1,0:T(8,128)(2,1)S(1)}, u32[]{:S(2)}, u32[]{:S(2)}) collective-permute-start(bf16[256,128]{1,0:T(8,128)(2,1)S(1)} %copy.130), channel_id=1, source_target_pairs={{14,0},{0,2},{2,4},{4,6},{6,8},{8,10},{10,12},{12,14},{15,1},{1,3}... | collective-permute-start | bytes 196616 | tf_op jit(solution)/shard_map/while/body/eval_jaxpr/ppermute | solution.py:22
  201.2 8.2 %collective-permute-start.4 = (bf16[256,128]{1,0:T(8,128)(2,1)S(1)}, bf16[256,128]{1,0:T(8,128)(2,1)S(1)}, u32[]{:S(2)}, u32[]{:S(2)}) collective-permute-start(bf16[256,128]{1,0:T(8,128)(2,1)S(1)} %copy.131), channel_id=1, source_target_pairs={{14,0},{0,2},{2,4},{4,6},{6,8},{8,10},{10,12},{12,14},{15,1},{1,3}... | collective-permute-start | bytes 196616 | tf_op jit(solution)/shard_map/while/body/eval_jaxpr/ppermute | solution.py:22
  215.3 8.0 %collective-permute-start.14 = (f32[256,128]{1,0:T(8,128)S(1)}, f32[256,128]{1,0:T(8,128)S(1)}, u32[]{:S(2)}, u32[]{:S(2)}) collective-permute-start(f32[256,128]{1,0:T(8,128)S(1)} %add.184), channel_id=1, source_target_pairs={{8,0},{10,2},{12,4},{14,6},{0,8},{2,10},{4,12},{6,14},{9,1},{11,3}... | collective-permute-start | bytes 393224 | tf_op jit(solution)/shard_map/ppermute | solution.py:22
  216.6 8.1 %collective-permute-start.13 = (f32[256,128]{1,0:T(8,128)S(1)}, f32[256,128]{1,0:T(8,128)S(1)}, u32[]{:S(2)}, u32[]{:S(2)}) collective-permute-start(f32[256,128]{1,0:T(8,128)S(1)} %add.183), channel_id=1, source_target_pairs={{8,0},{10,2},{12,4},{14,6},{0,8},{2,10},{4,12},{6,14},{9,1},{11,3}... | collective-permute-start | bytes 393224 | tf_op jit(solution)/shard_map/ppermute | solution.py:22
  (29 other events, 200.0 us)
Sparse Core Ops, SparseCore 0:
  225.5 17.0 all-reduce.2
where the time goes:
time: 253 us
  waiting for transfers between devices  140 us (55%)
  starting transfers between devices  42.1 us (17%)
  local copies, waits for them, and re-layouts  19.8 us (8%)
  between operations  15.7 us (6%)
  matrix products  13.7 us (5%)
  loops' own time  13.3 us (5%)
  other arithmetic  7.43 us (3%)
    ppermute x46, waiting for transfers between devices, from_behind(): return lax.ppermute(block, axis, route)  114 us
    ppermute x46, starting transfers between devices, from_behind(): return lax.ppermute(block, axis, route)  31.1 us
    psum x1, waiting for transfers between devices, per_device(): key_sum, value_sum = lax.psum(moving, 'head')  15.2 us
    ppermute x4, waiting for transfers between devices, shifted(): return lax.ppermute(value, axis, pairs)  11.4 us
    dynamic_slice x18, local copies, waits for them, and re-layouts, per_device(): lax.scan(stats_step, (start_block, stats), steps_all)  11.1 us
    ppermute x4, starting transfers between devices, shifted(): return lax.ppermute(value, axis, pairs)  10.9 us
    unnamed x17, local copies, waits for them, and re-layouts  6.14 us
  transfers between devices with their start and end apart: 51, of which 42 were waited for; matrix products, arithmetic and copies ran while one was open for 13% of the time, Pallas kernels for 0%

commit v1 on v0

v1 whole, which is shorter than its diff:
```python
import functools
import math

import jax
import jax.numpy as jnp
from jax import lax
from jax.experimental import pallas as pl
from jax.experimental.pallas import tpu as pltpu
from jax.sharding import PartitionSpec as P

HOPS = 2
DOC_CAP = 4096
NEG = -1e30
MESH = pl.DeviceIdType.MESH
F32 = jnp.float32
BF16 = jnp.bfloat16


def dot(a, b, dims):
    return lax.dot_general(a, b, (dims, ((), ())), preferred_element_type=F32)


def kernel(
    n, heads_n, reach, docs,
    q_ref, k_ref, v_ref, g_ref, doc_ref, plan_ref,
    out_ref, dq_ref, dk_ref, dv_ref,
    kbuf, vbuf, scores, wb_scr, qs, gs, qt, gt,
    dk_out, dv_out, dk_in, dv_in, dk_own, dv_own, sum_out, sum_in,
    stage, win, pick, picked, plan_own, plan_far,
    kv_s, kv_r, dk_s, dk_r, win_s, win_r, pick_s, pick_r, plan_s, plan_r, sum_s, sum_r,
):
    tok, dh = k_ref.shape
    width = q_ref.shape[1]
    hh = width // dh
    half = tok // 2
    me = lax.axis_index("ctx")
    my_head = lax.axis_index("head")
    partner = me + 1 - 2 * lax.rem(me, 2)
    inv_root = 1.0 / math.sqrt(dh)
    factor = inv_root * math.log2(math.e)
    far = max(reach, HOPS)

    barrier = pltpu.get_barrier_semaphore()
    count = heads_n - 1
    for d in range(1, far + 1):
        count = count + jnp.where(me + d < n, 1, 0) + jnp.where(me >= d, 1, 0)

        @pl.when(me + d < n)
        def _():
            pl.semaphore_signal(barrier, inc=1, device_id={"ctx": me + d}, device_id_type=MESH)

        @pl.when(me >= d)
        def _():
            pl.semaphore_signal(barrier, inc=1, device_id={"ctx": me - d}, device_id_type=MESH)

    for o in range(1, heads_n):
        pl.semaphore_signal(
            barrier, inc=1, device_id={"head": lax.rem(my_head + o, heads_n)}, device_id_type=MESH
        )
    row = lax.broadcasted_iota(jnp.int32, plan_own.shape, 0)
    plan_own[...] = jnp.where(row == 0, plan_ref[0], plan_ref[1]).astype(F32)
    pl.semaphore_wait(barrier, count)

    def ctx_copy(src, dst, s, r, target):
        return pltpu.make_async_remote_copy(
            src_ref=src, dst_ref=dst, send_sem=s, recv_sem=r,
            device_id={"ctx": target}, device_id_type=MESH,
        )

    def k_copy(d):
        return ctx_copy(k_ref, kbuf.at[d - 1], kv_s.at[0, d - 1], kv_r.at[0, d - 1], me + d)

    def v_copy(d):
        return ctx_copy(v_ref, vbuf.at[d - 1], kv_s.at[1, d - 1], kv_r.at[1, d - 1], me + d)

    def dk_copy(d):
        return ctx_copy(dk_out.at[d - 1], dk_in.at[d - 1], dk_s.at[0, d - 1], dk_r.at[0, d - 1], me - d)

    def dv_copy(d):
        return ctx_copy(dv_out.at[d - 1], dv_in.at[d - 1], dk_s.at[1, d - 1], dk_r.at[1, d - 1], me - d)

    def win_copy(a, side):
        target = me + HOPS if side == 0 else me - HOPS
        return ctx_copy(stage.at[a], win.at[a, side], win_s.at[a, side], win_r.at[a, side], target)

    def pick_copy(a):
        return ctx_copy(pick.at[a], picked.at[a], pick_s.at[a], pick_r.at[a], partner)

    plan_copy = ctx_copy(plan_own, plan_far, plan_s, plan_r, partner)

    for d in range(1, reach + 1):

        @pl.when(me + d < n)
        def _():
            k_copy(d).start()
            v_copy(d).start()

    plan_copy.start()

    for h in range(hh):
        cols = slice(h * dh, (h + 1) * dh)
        rows = slice(h * tok, (h + 1) * tok)
        qh = q_ref[:, cols]
        gh = g_ref[:, cols]
        qs[rows, :] = qh
        gs[rows, :] = gh
        qt[:, rows] = qh.T
        gt[:, rows] = gh.T

    lanes = hh * tok
    place = me * tok + lax.rem(lax.broadcasted_iota(jnp.int32, (1, lanes), 1), tok)
    start = jnp.zeros((1, lanes), jnp.int32)
    bound = jnp.int32(0)
    for j in range(docs):
        bound = bound + doc_ref[j]
        start = jnp.where(bound <= place, bound, start)
    offset = lax.broadcasted_iota(jnp.int32, (tok, lanes), 0)

    def keys(d):
        return k_ref[...] if d == 0 else kbuf[d - 1]

    def values(d):
        return v_ref[...] if d == 0 else vbuf[d - 1]

    top = jnp.full((1, lanes), NEG, F32)
    for d in range(reach + 1):
        if d:

            @pl.when(me >= d)
            def _():
                k_copy(d).wait_recv()

            @pl.when(me < d)
            def _():
                kbuf[d - 1] = jnp.zeros((tok, dh), BF16)
                vbuf[d - 1] = jnp.zeros((tok, dh), BF16)

        raw = dot(keys(d), qt[...], ((1,), (0,)))
        t = offset + (me - d) * tok
        allowed = t >= start
        if d == 0:
            allowed = allowed & (t <= place)
        else:
            allowed = allowed & (t >= 0)
        raw = jnp.where(allowed, raw, NEG)
        scores[d] = raw
        top = jnp.maximum(top, jnp.max(raw, axis=0, keepdims=True))

    total = jnp.zeros((1, lanes), F32)
    for d in range(reach + 1):
        e = jnp.exp2((scores[d] - top) * factor)
        scores[d] = e
        total = total + jnp.sum(e, axis=0, keepdims=True)
    inverse = 1.0 / total

    att = jnp.zeros((dh, lanes), F32)
    for d in range(reach, -1, -1):
        if d:

            @pl.when(me >= d)
            def _():
                v_copy(d).wait_recv()

        wb = (scores[d] * inverse).astype(BF16)
        att = att + dot(values(d), wb, ((0,), (0,)))
        wb_scr[d] = wb
    att = att.astype(BF16)
    for h in range(hh):
        stage[0, :, h * dh:(h + 1) * dh] = att[:, h * tok:(h + 1) * tok].T

    def send_window(a):
        @pl.when(me + HOPS < n)
        def _():
            win_copy(a, 0).start()

        @pl.when(me >= HOPS)
        def _():
            win_copy(a, 1).start()

    send_window(0)
    dots = jnp.sum(gt[...].astype(F32) * att.astype(F32), axis=0, keepdims=True)

    grad = jnp.zeros((dh, lanes), F32)
    for d in range(reach, -1, -1):
        value_term = dot(wb_scr[d], gs[...], ((1,), (0,)))
        gw = dot(values(d), gt[...], ((1,), (0,)))
        ds = (scores[d] * inverse * (gw - dots)).astype(BF16)
        key_term = dot(ds, qs[...], ((1,), (0,))) * inv_root
        grad = grad + dot(keys(d), ds, ((0,), (0,)))
        if d:
            dv_out[d - 1] = value_term.astype(BF16)
            dk_out[d - 1] = key_term.astype(BF16)

            @pl.when(me >= d)
            def _():
                dv_copy(d).start()
                dk_copy(d).start()

        else:
            dv_own[...] = value_term
            dk_own[...] = key_term
    grad = (grad * inv_root).astype(BF16)
    for h in range(hh):
        stage[1, :, h * dh:(h + 1) * dh] = grad[:, h * tok:(h + 1) * tok].T
    send_window(1)

    plan_copy.wait_recv()
    side = lax.rem(me, 2)
    other = me + HOPS - 2 * HOPS * side
    for a in range(2):

        @pl.when(me >= HOPS)
        def _():
            win_copy(a, 0).wait_recv()

        @pl.when(me + HOPS < n)
        def _():
            win_copy(a, 1).wait_recv()

        for s in range(2):
            want = plan_far[s:s + 1, :]
            acc = jnp.zeros((half, width), F32)
            for p in range(2):
                rows = slice(p * half, (p + 1) * half)
                own = jnp.broadcast_to(want == (2 * me + p).astype(F32), (half, width))
                acc = jnp.where(own, stage[a, rows, :].astype(F32), acc)
                away = jnp.broadcast_to(want == (2 * other + p).astype(F32), (half, width))
                acc = jnp.where(away, win[a, 1 - side, rows, :].astype(F32), acc)
            pick[a, s * half:(s + 1) * half, :] = acc.astype(BF16)
        pick_copy(a).start()

    for d in range(1, reach + 1):

        @pl.when(me + d < n)
        def _():
            dv_copy(d).wait_recv()
            dv_own[...] += dv_in[d - 1].astype(F32)
            dk_copy(d).wait_recv()
            dk_own[...] += dk_in[d - 1].astype(F32)

    sum_out[0] = dk_own[...]
    sum_out[1] = dv_own[...]

    def sum_copy(o):
        return pltpu.make_async_remote_copy(
            src_ref=sum_out, dst_ref=sum_in.at[o - 1], send_sem=sum_s.at[o - 1], recv_sem=sum_r.at[o - 1],
            device_id={"head": lax.rem(my_head + o, heads_n)}, device_id_type=MESH,
        )

    for o in range(1, heads_n):
        sum_copy(o).start()

    for a in range(2):
        pick_copy(a).wait_recv()
        for s in range(2):
            want = plan_own[s:s + 1, :]
            rows_s = slice(s * half, (s + 1) * half)
            acc = picked[a, rows_s, :].astype(F32)
            for p in range(2):
                rows = slice(p * half, (p + 1) * half)
                for base, at in ((0, None), (-HOPS, 0), (HOPS, 1)):
                    src = stage[a, rows, :] if at is None else win[a, at, rows, :]
                    hit = jnp.broadcast_to(want == (2 * (me + base) + p).astype(F32), (half, width))
                    acc = jnp.where(hit, src.astype(F32), acc)
            if a == 0:
                out_ref[rows_s, :] = acc.astype(BF16)
            else:
                dq_ref[rows_s, :] = acc

    for o in range(1, heads_n):
        sum_copy(o).wait_recv()
    dk_ref[...] = sum_out[0] + sum(sum_in[o, 0] for o in range(heads_n - 1))
    dv_ref[...] = sum_out[1] + sum(sum_in[o, 1] for o in range(heads_n - 1))

    for d in range(1, reach + 1):

        @pl.when(me + d < n)
        def _():
            k_copy(d).wait_send()
            v_copy(d).wait_send()

        @pl.when(me >= d)
        def _():
            dk_copy(d).wait_send()
            dv_copy(d).wait_send()

    for a in range(2):

        @pl.when(me + HOPS < n)
        def _():
            win_copy(a, 0).wait_send()

        @pl.when(me >= HOPS)
        def _():
            win_copy(a, 1).wait_send()

        pick_copy(a).wait_send()
    plan_copy.wait_send()
    for o in range(1, heads_n):
        sum_copy(o).wait_send()


def per_device(queries, key_input, value_input, grad_out, doc_lengths, stretch_plan):
    tok, dh = key_input.shape
    width = queries.shape[1]
    hh = width // dh
    n = lax.axis_size("ctx")
    heads_n = lax.axis_size("head")
    reach = min(n - 1, min(DOC_CAP, tok * n // 4) // tok)
    docs = doc_lengths.shape[0]
    lanes = hh * tok
    vmem = pl.BlockSpec(memory_space=pltpu.VMEM)
    smem = pl.BlockSpec(memory_space=pltpu.SMEM)
    dma = pltpu.SemaphoreType.DMA
    return pl.pallas_call(
        functools.partial(kernel, n, heads_n, reach, docs),
        out_shape=(
            jax.ShapeDtypeStruct((tok, width), BF16),
            jax.ShapeDtypeStruct((tok, width), F32),
            jax.ShapeDtypeStruct((tok, dh), F32),
            jax.ShapeDtypeStruct((tok, dh), F32),
        ),
        in_specs=[vmem, vmem, vmem, vmem, smem, smem],
        out_specs=(vmem, vmem, vmem, vmem),
        scratch_shapes=[
            pltpu.VMEM((reach, tok, dh), BF16),
            pltpu.VMEM((reach, tok, dh), BF16),
            pltpu.VMEM((reach + 1, tok, lanes), F32),
            pltpu.VMEM((reach + 1, tok, lanes), BF16),
            pltpu.VMEM((lanes, dh), BF16),
            pltpu.VMEM((lanes, dh), BF16),
            pltpu.VMEM((dh, lanes), BF16),
            pltpu.VMEM((dh, lanes), BF16),
            pltpu.VMEM((reach, tok, dh), BF16),
            pltpu.VMEM((reach, tok, dh), BF16),
            pltpu.VMEM((reach, tok, dh), BF16),
            pltpu.VMEM((reach, tok, dh), BF16),
            pltpu.VMEM((tok, dh), F32),
            pltpu.VMEM((tok, dh), F32),
            pltpu.VMEM((2, tok, dh), F32),
            pltpu.VMEM((heads_n - 1, 2, tok, dh), F32),
            pltpu.VMEM((2, tok, width), BF16),
            pltpu.VMEM((2, 2, tok, width), BF16),
            pltpu.VMEM((2, tok, width), BF16),
            pltpu.VMEM((2, tok, width), BF16),
            pltpu.VMEM((8, width), F32),
            pltpu.VMEM((8, width), F32),
            dma((2, reach)), dma((2, reach)),
            dma((2, reach)), dma((2, reach)),
            dma((2, 2)), dma((2, 2)),
            dma((2,)), dma((2,)),
            dma, dma,
            dma((heads_n - 1,)), dma((heads_n - 1,)),
        ],
        compiler_params=pltpu.CompilerParams(
            collective_id=0, has_side_effects=True, vmem_limit_bytes=48 * 1024 * 1024
        ),
    )(queries, key_input, value_input, grad_out, doc_lengths, stretch_plan)


def solution(mesh):
    return jax.shard_map(
        per_device,
        mesh=mesh,
        in_specs=(
            P(("groups", "ctx"), "head"),
            P(("groups", "ctx"), None),
            P(("groups", "ctx"), None),
            P(("groups", "ctx"), "head"),
            P("groups"),
            P(("groups", "ctx")),
        ),
        out_specs=(
            P(("groups", "ctx"), "head"),
            P(("groups", "ctx"), "head"),
            P(("groups", "ctx"), None),
            P(("groups", "ctx"), None),
        ),
        check_vma=False,
    )
```

time: 253 us -> 33.7 us (0.13)
  waiting for transfers between devices: 140 us -> 0 us
  starting transfers between devices: 42.1 us -> 0 us
  Pallas kernels: 0 us -> 25.3 us
  between operations: 15.7 us -> 0.66 us
  matrix products: 13.7 us -> 0 us
  loops' own time: 13.3 us -> 0 us
  local copies, waits for them, and re-layouts: 19.8 us -> 7.46 us
  other arithmetic: 7.43 us -> 0 us
    ppermute x50 -> x0, waiting for transfers between devices: 125 us -> none  [the longest x46 114 us: from_behind(): return lax.ppermute(block, axis, route)]
    ppermute x50 -> x0, starting transfers between devices: 42.1 us -> none  [the longest x46 31.1 us: from_behind(): return lax.ppermute(block, axis, route)]
    pallas_call x0 -> x1, Pallas kernels: none -> 25.3 us  [per_device(): pl.pallas_call(functools.partial(kernel, n, heads_n, reach, docs), out_sh...]
    psum x1 -> x0, waiting for transfers between devices: 15.2 us -> none  [per_device(): key_sum, value_sum = lax.psum(moving, 'head')]
    dot_general x49 -> x0, matrix products: 13.7 us -> none  [the longest x14 3.68 us: masked_scores(): jnp.einsum('phd,td->pht', query_heads, block_keys, preferred_element_type...]
    another operation x3 -> x0, loops' own time: 13.3 us -> none  [the longest x1 4.55 us: per_device(): lax.scan(stats_step, (start_block, stats), steps_all)]
    dynamic_slice x19 -> x0, local copies, waits for them, and re-layouts: 11.1 us -> none  [the longest x18 11.1 us: per_device(): lax.scan(stats_step, (start_block, stats), steps_all)]
    and x19 -> x0, other arithmetic: 2.7 us -> none  [block_mask(): return same_doc & inside]
  transfers between devices with their start and end apart: 51 -> 0, of which waited for: 42 -> 0; matrix products, arithmetic and copies ran while one was open for 13% -> 0% of each run, Pallas kernels for 0% -> 0%
where the time goes in v1:
time: 33.7 us; the launch traced here: 33.4 us
  Pallas kernels  25.3 us (75%)
  local copies, waits for them, and re-layouts  7.46 us (22%)
  between operations  0.66 us (2%)
    pallas_call x1, Pallas kernels, per_device(): pl.pallas_call(functools.partial(kernel, n, heads_n, reach, docs), out_sh...  25.3 us
    unnamed x16, local copies, waits for them, and re-layouts  7.46 us

profile of v1, /device:TPU:0, one launch (start us, length us, event | category | flops | bytes accessed | tf_op | source)
XLA Modules:
  0.0 33.4 jit_solution(10243301703962122226)
XLA Ops:
  0.6 0.0 copy-start
  0.6 0.9 %copy-done = bf16[256,256]{1,0:T(8,128)(2,1)S(1)} copy-done((bf16[256,256]{1,0:T(8,128)(2,1)S(1)}, bf16[256,256]{1,0:T(8,128)(2,1)}, u32[]{:S(2)}) %copy-start) | copy-done | bytes 131096
  1.5 0.0 copy-start.1
  1.5 0.9 %copy-done.1 = bf16[256,256]{1,0:T(8,128)(2,1)S(1)} copy-done((bf16[256,256]{1,0:T(8,128)(2,1)S(1)}, bf16[256,256]{1,0:T(8,128)(2,1)}, u32[]{:S(2)}) %copy-start.1) | copy-done | bytes 131096
  2.4 0.0 copy-start.2
  2.4 0.8 %copy-done.2 = bf16[256,128]{1,0:T(8,128)(2,1)S(1)} copy-done((bf16[256,128]{1,0:T(8,128)(2,1)S(1)}, bf16[256,128]{1,0:T(8,128)(2,1)}, u32[]{:S(2)}) %copy-start.2) | copy-done | bytes 65560
  3.3 0.0 copy-start.3
  3.3 0.8 %copy-done.3 = bf16[256,128]{1,0:T(8,128)(2,1)S(1)} copy-done((bf16[256,128]{1,0:T(8,128)(2,1)S(1)}, bf16[256,128]{1,0:T(8,128)(2,1)}, u32[]{:S(2)}) %copy-start.3) | copy-done | bytes 65560
  4.1 0.0 copy-start.4
  4.1 0.7 %copy-done.4 = s32[16]{0:T(128)S(1)} copy-done((s32[16]{0:T(128)S(1)}, s32[16]{0:T(128)}, u32[]{:S(2)}) %copy-start.4) | copy-done | bytes 88
  4.8 0.0 copy-start.5
  4.8 0.7 %copy-done.5 = s32[2]{0:T(128)S(1)} copy-done((s32[2]{0:T(128)S(1)}, s32[2]{0:T(128)}, u32[]{:S(2)}) %copy-start.5) | copy-done | bytes 32
  5.4 25.3 %shard_map.93 = (bf16[256,256]{1,0:T(8,128)(2,1)S(1)}, f32[256,256]{1,0:T(8,128)S(1)}, f32[256,128]{1,0:T(8,128)S(1)}, f32[256,128]{1,0:T(8,128)S(1)}) custom-call(bf16[256,256]{1,0:T(8,128)(2,1)S(1)} %copy-done, bf16[256,128]{1,0:T(8,128)(2,1)S(1)} %copy-done.2, bf16[256,128]{1,0:T(8,128)(2,1)S(1)} %copy-done.3, bf16[256,256]{1,0:T(8,128)(2,1)S(1)} %copy-done.1, ...), custom_call_target="tpu_custom_call" | custom-call | tf_op jit(solution)/shard_map/pallas_call | solution.py:315
  30.8 0.7 %copy.14 = bf16[256,256]{1,0:T(8,128)(2,1)} copy(bf16[256,256]{1,0:T(8,128)(2,1)S(1)} %get-tuple-element.8) | data formatting | bytes 262144
  31.4 0.7 %copy.15 = f32[256,256]{1,0:T(8,128)} copy(f32[256,256]{1,0:T(8,128)S(1)} %get-tuple-element.9) | data formatting | bytes 524288
  32.1 0.7 %copy.16 = f32[256,128]{1,0:T(8,128)} copy(f32[256,128]{1,0:T(8,128)S(1)} %get-tuple-element.10) | data formatting | bytes 262144
  32.8 0.7 %copy.17 = f32[256,128]{1,0:T(8,128)} copy(f32[256,128]{1,0:T(8,128)S(1)} %get-tuple-element.11) | data formatting | bytes 262144
Async XLA Ops:
  0.6 0.9 %copy-start = (bf16[256,256]{1,0:T(8,128)(2,1)S(1)}, bf16[256,256]{1,0:T(8,128)(2,1)}, u32[]{:S(2)}) copy-start(bf16[256,256]{1,0:T(8,128)(2,1)} %q_ref.1) | copy-start | bytes 393220
  1.5 0.9 %copy-start.1 = (bf16[256,256]{1,0:T(8,128)(2,1)S(1)}, bf16[256,256]{1,0:T(8,128)(2,1)}, u32[]{:S(2)}) copy-start(bf16[256,256]{1,0:T(8,128)(2,1)} %g_ref.1) | copy-start | bytes 393220
  2.4 0.8 %copy-start.2 = (bf16[256,128]{1,0:T(8,128)(2,1)S(1)}, bf16[256,128]{1,0:T(8,128)(2,1)}, u32[]{:S(2)}) copy-start(bf16[256,128]{1,0:T(8,128)(2,1)} %k_ref.1) | copy-start | bytes 196612
  3.3 0.8 %copy-start.3 = (bf16[256,128]{1,0:T(8,128)(2,1)S(1)}, bf16[256,128]{1,0:T(8,128)(2,1)}, u32[]{:S(2)}) copy-start(bf16[256,128]{1,0:T(8,128)(2,1)} %v_ref.1) | copy-start | bytes 196612
  4.1 0.7 %copy-start.4 = (s32[16]{0:T(128)S(1)}, s32[16]{0:T(128)}, u32[]{:S(2)}) copy-start(s32[16]{0:T(128)} %doc_ref.1) | copy-start | bytes 196
  4.8 0.7 %copy-start.5 = (s32[2]{0:T(128)S(1)}, s32[2]{0:T(128)}, u32[]{:S(2)}) copy-start(s32[2]{0:T(128)} %plan_ref.1) | copy-start | bytes 28

commit v2 on v1

--- a/solution.py
+++ b/solution.py
@@ -10,6 +10,7 @@
 
 HOPS = 2
 DOC_CAP = 4096
+VMEM_GRANT = 64000 * 1024
 NEG = -1e30
 MESH = pl.DeviceIdType.MESH
 F32 = jnp.float32
@@ -22,11 +23,13 @@
 
 def kernel(
     n, heads_n, reach, docs,
-    q_ref, k_ref, v_ref, g_ref, doc_ref, plan_ref,
-    out_ref, dq_ref, dk_ref, dv_ref,
+    q_hbm, k_hbm, v_hbm, g_hbm, doc_hbm, plan_hbm,
+    out_hbm, dq_hbm, dk_hbm, dv_hbm,
+    out_ref, dq_ref, dk_ref, dv_ref, store_s,
     kbuf, vbuf, scores, wb_scr, qs, gs, qt, gt,
     dk_out, dv_out, dk_in, dv_in, dk_own, dv_own, sum_out, sum_in,
     stage, win, pick, picked, plan_own, plan_far,
+    q_ref, k_ref, v_ref, g_ref, doc_ref, plan_ref, load_s,
     kv_s, kv_r, dk_s, dk_r, win_s, win_r, pick_s, pick_r, plan_s, plan_r, sum_s, sum_r,
 ):
     tok, dh = k_ref.shape
@@ -40,6 +43,16 @@
     factor = inv_root * math.log2(math.e)
     far = max(reach, HOPS)
 
+    loads = [
+        pltpu.make_async_copy(src, dst, load_s.at[j])
+        for j, (src, dst) in enumerate((
+            (plan_hbm, plan_ref), (doc_hbm, doc_ref), (q_hbm, q_ref),
+            (g_hbm, g_ref), (k_hbm, k_ref), (v_hbm, v_ref),
+        ))
+    ]
+    for load in loads:
+        load.start()
+
     barrier = pltpu.get_barrier_semaphore()
     count = heads_n - 1
     for d in range(1, far + 1):
@@ -57,8 +70,6 @@
         pl.semaphore_signal(
             barrier, inc=1, device_id={"head": lax.rem(my_head + o, heads_n)}, device_id_type=MESH
         )
-    row = lax.broadcasted_iota(jnp.int32, plan_own.shape, 0)
-    plan_own[...] = jnp.where(row == 0, plan_ref[0], plan_ref[1]).astype(F32)
     pl.semaphore_wait(barrier, count)
 
     def ctx_copy(src, dst, s, r, target):
@@ -68,10 +79,10 @@
         )
 
     def k_copy(d):
-        return ctx_copy(k_ref, kbuf.at[d - 1], kv_s.at[0, d - 1], kv_r.at[0, d - 1], me + d)
+        return ctx_copy(k_hbm, kbuf.at[d - 1], kv_s.at[0, d - 1], kv_r.at[0, d - 1], me + d)
 
     def v_copy(d):
-        return ctx_copy(v_ref, vbuf.at[d - 1], kv_s.at[1, d - 1], kv_r.at[1, d - 1], me + d)
+        return ctx_copy(v_hbm, vbuf.at[d - 1], kv_s.at[1, d - 1], kv_r.at[1, d - 1], me + d)
 
     def dk_copy(d):
         return ctx_copy(dk_out.at[d - 1], dk_in.at[d - 1], dk_s.at[0, d - 1], dk_r.at[0, d - 1], me - d)
@@ -93,8 +104,17 @@
         @pl.when(me + d < n)
         def _():
             k_copy(d).start()
+
+    for d in range(1, reach + 1):
+
+        @pl.when(me + d < n)
+        def _():
             v_copy(d).start()
 
+    for load in loads:
+        load.wait()
+    row = lax.broadcasted_iota(jnp.int32, plan_own.shape, 0)
+    plan_own[...] = jnp.where(row == 0, plan_ref[0], plan_ref[1]).astype(F32)
     plan_copy.start()
 
     for h in range(hh):
@@ -249,6 +269,12 @@
 
     for o in range(1, heads_n):
         sum_copy(o).start()
+    stores = [
+        pltpu.make_async_copy(src, dst, store_s.at[j])
+        for j, (src, dst) in enumerate((
+            (out_ref, out_hbm), (dq_ref, dq_hbm), (dk_ref, dk_hbm), (dv_ref, dv_hbm),
+        ))
+    ]
 
     for a in range(2):
         pick_copy(a).wait_recv()
@@ -266,11 +292,14 @@
                 out_ref[rows_s, :] = acc.astype(BF16)
             else:
                 dq_ref[rows_s, :] = acc
+        stores[a].start()
 
     for o in range(1, heads_n):
         sum_copy(o).wait_recv()
     dk_ref[...] = sum_out[0] + sum(sum_in[o, 0] for o in range(heads_n - 1))
+    stores[2].start()
     dv_ref[...] = sum_out[1] + sum(sum_in[o, 1] for o in range(heads_n - 1))
+    stores[3].start()
 
     for d in range(1, reach + 1):
 
@@ -298,6 +327,19 @@
     plan_copy.wait_send()
     for o in range(1, heads_n):
         sum_copy(o).wait_send()
+    for store in stores:
+        store.wait()
+
+
+def write_out(a, b, c, d, a_out, b_out, c_out, d_out, sems):
+    copies = [
+        pltpu.make_async_copy(src, dst, sems.at[j])
+        for j, (src, dst) in enumerate(((a, a_out), (b, b_out), (c, c_out), (d, d_out)))
+    ]
+    for copy in copies:
+        copy.start()
+    for copy in copies:
+        copy.wait()
 
 
 def per_device(queries, key_input, value_input, grad_out, doc_lengths, stretch_plan):
@@ -309,20 +351,25 @@
     reach = min(n - 1, min(DOC_CAP, tok * n // 4) // tok)
     docs = doc_lengths.shape[0]
     lanes = hh * tok
-    vmem = pl.BlockSpec(memory_space=pltpu.VMEM)
-    smem = pl.BlockSpec(memory_space=pltpu.SMEM)
+    hbm = pl.BlockSpec(memory_space=pltpu.HBM)
     dma = pltpu.SemaphoreType.DMA
-    return pl.pallas_call(
+    results = (
+        jax.ShapeDtypeStruct((tok, width), BF16),
+        jax.ShapeDtypeStruct((tok, width), F32),
+        jax.ShapeDtypeStruct((tok, dh), F32),
+        jax.ShapeDtypeStruct((tok, dh), F32),
+    )
+    held = pl.pallas_call(
         functools.partial(kernel, n, heads_n, reach, docs),
-        out_shape=(
-            jax.ShapeDtypeStruct((tok, width), BF16),
-            jax.ShapeDtypeStruct((tok, width), F32),
-            jax.ShapeDtypeStruct((tok, dh), F32),
-            jax.ShapeDtypeStruct((tok, dh), F32),
-        ),
-        in_specs=[vmem, vmem, vmem, vmem, smem, smem],
-        out_specs=(vmem, vmem, vmem, vmem),
+        out_shape=results,
+        in_specs=[hbm] * 6,
+        out_specs=(hbm,) * 4,
         scratch_shapes=[
+            pltpu.VMEM((tok, width), BF16),
+            pltpu.VMEM((tok, width), F32),
+            pltpu.VMEM((tok, dh), F32),
+            pltpu.VMEM((tok, dh), F32),
+            dma((4,)),
             pltpu.VMEM((reach, tok, dh), BF16),
             pltpu.VMEM((reach, tok, dh), BF16),
             pltpu.VMEM((reach + 1, tok, lanes), F32),
@@ -345,6 +392,13 @@
             pltpu.VMEM((2, tok, width), BF16),
             pltpu.VMEM((8, width), F32),
             pltpu.VMEM((8, width), F32),
+            pltpu.VMEM((tok, width), BF16),
+            pltpu.VMEM((tok, dh), BF16),
+            pltpu.VMEM((tok, dh), BF16),
+            pltpu.VMEM((tok, width), BF16),
+            pltpu.SMEM((docs,), jnp.int32),
+            pltpu.SMEM((2,), jnp.int32),
+            dma((6,)),
             dma((2, reach)), dma((2, reach)),
             dma((2, reach)), dma((2, reach)),
             dma((2, 2)), dma((2, 2)),
@@ -353,9 +407,17 @@
             dma((heads_n - 1,)), dma((heads_n - 1,)),
         ],
         compiler_params=pltpu.CompilerParams(
-            collective_id=0, has_side_effects=True, vmem_limit_bytes=48 * 1024 * 1024
+            collective_id=0, has_side_effects=True, vmem_limit_bytes=VMEM_GRANT
         ),
     )(queries, key_input, value_input, grad_out, doc_lengths, stretch_plan)
+    return pl.pallas_call(
+        write_out,
+        out_shape=results,
+        in_specs=[pl.BlockSpec(memory_space=pl.ANY)] * 4,
+        out_specs=(hbm,) * 4,
+        scratch_shapes=[dma((4,))],
+        compiler_params=pltpu.CompilerParams(vmem_limit_bytes=VMEM_GRANT),
+    )(*held)
 
 
 def solution(mesh):

time: 33.7 us -> 47.4 us (1.41)
  Pallas kernels: 25.3 us -> 46.6 us
  local copies, waits for them, and re-layouts: 7.46 us -> 0 us
    pallas_call x0 -> x1, Pallas kernels: none -> 21 us  [per_device(): pl.pallas_call(write_out, out_shape=results, in_specs=[pl.BlockSpec(memor...]
    unnamed x16 -> x0, local copies, waits for them, and re-layouts: 7.46 us -> none
where the time goes in v2:
time: 47.4 us; the launch traced here: 47.2 us
  Pallas kernels  46.6 us (98%)
  between operations  0.64 us (1%)
    pallas_call x1, Pallas kernels, per_device(): pl.pallas_call(functools.partial(kernel, n, heads_n, reach, docs), out_sh...  25.6 us
    pallas_call x1, Pallas kernels, per_device(): pl.pallas_call(write_out, out_shape=results, in_specs=[pl.BlockSpec(memor...  21 us

profile of v2, /device:TPU:0, one launch (start us, length us, event | category | flops | bytes accessed | tf_op | source)
XLA Modules:
  0.0 47.2 jit_solution(17654063226127416989)
XLA Ops:
  0.6 25.6 %shard_map.93 = (bf16[256,256]{1,0:T(8,128)(2,1)}, f32[256,256]{1,0:T(8,128)}, f32[256,128]{1,0:T(8,128)}, f32[256,128]{1,0:T(8,128)}) custom-call(bf16[256,256]{1,0:T(8,128)(2,1)} %q_hbm.1, bf16[256,128]{1,0:T(8,128)(2,1)} %k_hbm.1, bf16[256,128]{1,0:T(8,128)(2,1)} %v_hbm.1, bf16[256,256]{1,0:T(8,128)(2,1)} %g_hbm.1, s32[16]{0:T(128)} %doc_hbm.1, s32[2]{0:T(128)} %plan_hbm.1), custom_call_target="tpu_custom_call" | custom-call | tf_op jit(solution)/shard_map/pallas_call | solution.py:362
  26.2 21.0 %shard_map.94 = (bf16[256,256]{1,0:T(8,128)(2,1)}, f32[256,256]{1,0:T(8,128)}, f32[256,128]{1,0:T(8,128)}, f32[256,128]{1,0:T(8,128)}) custom-call(bf16[256,256]{1,0:T(8,128)(2,1)} %get-tuple-element.8.a, f32[256,256]{1,0:T(8,128)} %get-tuple-element.9.b, f32[256,128]{1,0:T(8,128)} %get-tuple-element.10.c, f32[256,128]{1,0:T(8,128)} %get-tuple-element.11.d), custom_call_target="tpu_custom_call" | custom-call | tf_op jit(solution)/shard_map/pallas_call | solution.py:413

commit v3 on v2

--- a/solution.py
+++ b/solution.py
@@ -25,12 +25,12 @@
     n, heads_n, reach, docs,
     q_hbm, k_hbm, v_hbm, g_hbm, doc_hbm, plan_hbm,
     out_hbm, dq_hbm, dk_hbm, dv_hbm,
-    out_ref, dq_ref, dk_ref, dv_ref, store_s,
+    out_ref, dq_ref, store_s,
     kbuf, vbuf, scores, wb_scr, qs, gs, qt, gt,
-    dk_out, dv_out, dk_in, dv_in, dk_own, dv_own, sum_out, sum_in,
+    part, part_in, red_out, red_in, sums,
     stage, win, pick, picked, plan_own, plan_far,
     q_ref, k_ref, v_ref, g_ref, doc_ref, plan_ref, load_s,
-    kv_s, kv_r, dk_s, dk_r, win_s, win_r, pick_s, pick_r, plan_s, plan_r, sum_s, sum_r,
+    kv_s, kv_r, part_s, part_r, red_s, red_r, win_s, win_r, pick_s, pick_r, plan_s, plan_r, sum_s, sum_r,
 ):
     tok, dh = k_ref.shape
     width = q_ref.shape[1]
@@ -84,19 +84,26 @@
     def v_copy(d):
         return ctx_copy(v_hbm, vbuf.at[d - 1], kv_s.at[1, d - 1], kv_r.at[1, d - 1], me + d)
 
-    def dk_copy(d):
-        return ctx_copy(dk_out.at[d - 1], dk_in.at[d - 1], dk_s.at[0, d - 1], dk_r.at[0, d - 1], me - d)
-
-    def dv_copy(d):
-        return ctx_copy(dv_out.at[d - 1], dv_in.at[d - 1], dk_s.at[1, d - 1], dk_r.at[1, d - 1], me - d)
-
-    def win_copy(a, side):
+    def head_copy(src, dst, s, r):
+        return pltpu.make_async_remote_copy(
+            src_ref=src, dst_ref=dst, send_sem=s, recv_sem=r,
+            device_id={"head": 1 - my_head}, device_id_type=MESH,
+        )
+
+    def part_copy(d):
+        return head_copy(part.at[d, 1 - my_head], part_in.at[d], part_s.at[d], part_r.at[d])
+
+    def red_copy(d):
+        return ctx_copy(red_out.at[d - 1], red_in.at[d - 1], red_s.at[d - 1], red_r.at[d - 1], me - d)
+
+    def win_copy(c, side):
         target = me + HOPS if side == 0 else me - HOPS
-        return ctx_copy(stage.at[a], win.at[a, side], win_s.at[a, side], win_r.at[a, side], target)
-
-    def pick_copy(a):
-        return ctx_copy(pick.at[a], picked.at[a], pick_s.at[a], pick_r.at[a], partner)
-
+        return ctx_copy(stage.at[c], win.at[c, side], win_s.at[c, side], win_r.at[c, side], target)
+
+    def pick_copy(c):
+        return ctx_copy(pick.at[c], picked.at[c], pick_s.at[c], pick_r.at[c], partner)
+
+    sum_copy = head_copy(sums.at[my_head], sums.at[my_head], sum_s, sum_r)
     plan_copy = ctx_copy(plan_own, plan_far, plan_s, plan_r, partner)
 
     for d in range(1, reach + 1):
@@ -185,19 +192,20 @@
         att = att + dot(values(d), wb, ((0,), (0,)))
         wb_scr[d] = wb
     att = att.astype(BF16)
+
+    def send_window(c, rows):
+        stage[c] = rows
+
+        @pl.when(me + HOPS < n)
+        def _():
+            win_copy(c, 0).start()
+
+        @pl.when(me >= HOPS)
+        def _():
+            win_copy(c, 1).start()
+
     for h in range(hh):
-        stage[0, :, h * dh:(h + 1) * dh] = att[:, h * tok:(h + 1) * tok].T
-
-    def send_window(a):
-        @pl.when(me + HOPS < n)
-        def _():
-            win_copy(a, 0).start()
-
-        @pl.when(me >= HOPS)
-        def _():
-            win_copy(a, 1).start()
-
-    send_window(0)
+        send_window(h, att[:, h * tok:(h + 1) * tok].T)
     dots = jnp.sum(gt[...].astype(F32) * att.astype(F32), axis=0, keepdims=True)
 
     grad = jnp.zeros((dh, lanes), F32)
@@ -207,98 +215,85 @@
         ds = (scores[d] * inverse * (gw - dots)).astype(BF16)
         key_term = dot(ds, qs[...], ((1,), (0,))) * inv_root
         grad = grad + dot(keys(d), ds, ((0,), (0,)))
-        if d:
-            dv_out[d - 1] = value_term.astype(BF16)
-            dk_out[d - 1] = key_term.astype(BF16)
-
-            @pl.when(me >= d)
-            def _():
-                dv_copy(d).start()
-                dk_copy(d).start()
-
-        else:
-            dv_own[...] = value_term
-            dk_own[...] = key_term
+        part[d, 0] = key_term
+        part[d, 1] = value_term
+        part_copy(d).start()
+    for d in range(reach, 0, -1):
+        part_copy(d).wait_recv()
+        red_out[d - 1] = (part[d, my_head] + part_in[d]).astype(BF16)
+
+        @pl.when(me >= d)
+        def _():
+            red_copy(d).start()
+
     grad = (grad * inv_root).astype(BF16)
     for h in range(hh):
-        stage[1, :, h * dh:(h + 1) * dh] = grad[:, h * tok:(h + 1) * tok].T
-    send_window(1)
+        send_window(hh + h, grad[:, h * tok:(h + 1) * tok].T)
 
     plan_copy.wait_recv()
     side = lax.rem(me, 2)
     other = me + HOPS - 2 * HOPS * side
-    for a in range(2):
+    for c in range(2 * hh):
 
         @pl.when(me >= HOPS)
         def _():
-            win_copy(a, 0).wait_recv()
+            win_copy(c, 0).wait_recv()
 
         @pl.when(me + HOPS < n)
         def _():
-            win_copy(a, 1).wait_recv()
+            win_copy(c, 1).wait_recv()
 
         for s in range(2):
             want = plan_far[s:s + 1, :]
-            acc = jnp.zeros((half, width), F32)
+            acc = jnp.zeros((half, dh), F32)
             for p in range(2):
                 rows = slice(p * half, (p + 1) * half)
-                own = jnp.broadcast_to(want == (2 * me + p).astype(F32), (half, width))
-                acc = jnp.where(own, stage[a, rows, :].astype(F32), acc)
-                away = jnp.broadcast_to(want == (2 * other + p).astype(F32), (half, width))
-                acc = jnp.where(away, win[a, 1 - side, rows, :].astype(F32), acc)
-            pick[a, s * half:(s + 1) * half, :] = acc.astype(BF16)
-        pick_copy(a).start()
-
+                own = jnp.broadcast_to(want == (2 * me + p).astype(F32), (half, dh))
+                acc = jnp.where(own, stage[c, rows, :].astype(F32), acc)
+                away = jnp.broadcast_to(want == (2 * other + p).astype(F32), (half, dh))
+                acc = jnp.where(away, win[c, 1 - side, rows, :].astype(F32), acc)
+            pick[c, s * half:(s + 1) * half, :] = acc.astype(BF16)
+        pick_copy(c).start()
+
+    part_copy(0).wait_recv()
+    sums[my_head] = part[0, my_head] + part_in[0]
     for d in range(1, reach + 1):
 
         @pl.when(me + d < n)
         def _():
-            dv_copy(d).wait_recv()
-            dv_own[...] += dv_in[d - 1].astype(F32)
-            dk_copy(d).wait_recv()
-            dk_own[...] += dk_in[d - 1].astype(F32)
-
-    sum_out[0] = dk_own[...]
-    sum_out[1] = dv_own[...]
-
-    def sum_copy(o):
-        return pltpu.make_async_remote_copy(
-            src_ref=sum_out, dst_ref=sum_in.at[o - 1], send_sem=sum_s.at[o - 1], recv_sem=sum_r.at[o - 1],
-            device_id={"head": lax.rem(my_head + o, heads_n)}, device_id_type=MESH,
-        )
-
-    for o in range(1, heads_n):
-        sum_copy(o).start()
+            red_copy(d).wait_recv()
+            sums[my_head] += red_in[d - 1].astype(F32)
+
+    sum_copy.start()
     stores = [
         pltpu.make_async_copy(src, dst, store_s.at[j])
         for j, (src, dst) in enumerate((
-            (out_ref, out_hbm), (dq_ref, dq_hbm), (dk_ref, dk_hbm), (dv_ref, dv_hbm),
+            (out_ref, out_hbm), (dq_ref, dq_hbm), (sums.at[0], dk_hbm), (sums.at[1], dv_hbm),
         ))
     ]
 
-    for a in range(2):
-        pick_copy(a).wait_recv()
+    for c in range(2 * hh):
+        pick_copy(c).wait_recv()
+        cols = slice((c % hh) * dh, (c % hh + 1) * dh)
         for s in range(2):
             want = plan_own[s:s + 1, :]
             rows_s = slice(s * half, (s + 1) * half)
-            acc = picked[a, rows_s, :].astype(F32)
+            acc = picked[c, rows_s, :].astype(F32)
             for p in range(2):
                 rows = slice(p * half, (p + 1) * half)
                 for base, at in ((0, None), (-HOPS, 0), (HOPS, 1)):
-                    src = stage[a, rows, :] if at is None else win[a, at, rows, :]
-                    hit = jnp.broadcast_to(want == (2 * (me + base) + p).astype(F32), (half, width))
+                    src = stage[c, rows, :] if at is None else win[c, at, rows, :]
+                    hit = jnp.broadcast_to(want == (2 * (me + base) + p).astype(F32), (half, dh))
                     acc = jnp.where(hit, src.astype(F32), acc)
-            if a == 0:
-                out_ref[rows_s, :] = acc.astype(BF16)
+            if c < hh:
+                out_ref[rows_s, cols] = acc.astype(BF16)
             else:
-                dq_ref[rows_s, :] = acc
-        stores[a].start()
-
-    for o in range(1, heads_n):
-        sum_copy(o).wait_recv()
-    dk_ref[...] = sum_out[0] + sum(sum_in[o, 0] for o in range(heads_n - 1))
+                dq_ref[rows_s, cols] = acc
+        if c == hh - 1:
+            stores[0].start()
+    stores[1].start()
+    sum_copy.wait_recv()
     stores[2].start()
-    dv_ref[...] = sum_out[1] + sum(sum_in[o, 1] for o in range(heads_n - 1))
     stores[3].start()
 
     for d in range(1, reach + 1):
@@ -310,35 +305,42 @@
 
         @pl.when(me >= d)
         def _():
-            dk_copy(d).wait_send()
-            dv_copy(d).wait_send()
-
-    for a in range(2):
+            red_copy(d).wait_send()
+
+    for d in range(reach + 1):
+        part_copy(d).wait_send()
+    for c in range(2 * hh):
 
         @pl.when(me + HOPS < n)
         def _():
-            win_copy(a, 0).wait_send()
+            win_copy(c, 0).wait_send()
 
         @pl.when(me >= HOPS)
         def _():
-            win_copy(a, 1).wait_send()
-
-        pick_copy(a).wait_send()
+            win_copy(c, 1).wait_send()
+
+        pick_copy(c).wait_send()
     plan_copy.wait_send()
-    for o in range(1, heads_n):
-        sum_copy(o).wait_send()
+    sum_copy.wait_send()
     for store in stores:
         store.wait()
 
 
-def write_out(a, b, c, d, a_out, b_out, c_out, d_out, sems):
-    copies = [
-        pltpu.make_async_copy(src, dst, sems.at[j])
-        for j, (src, dst) in enumerate(((a, a_out), (b, b_out), (c, c_out), (d, d_out)))
+def write_out(a, b, c, d, a_out, b_out, c_out, d_out, a_buf, b_buf, c_buf, d_buf, in_sems, out_sems):
+    ins = [
+        pltpu.make_async_copy(src, dst, in_sems.at[j])
+        for j, (src, dst) in enumerate(((a, a_buf), (b, b_buf), (c, c_buf), (d, d_buf)))
     ]
-    for copy in copies:
+    outs = [
+        pltpu.make_async_copy(src, dst, out_sems.at[j])
+        for j, (src, dst) in enumerate(((a_buf, a_out), (b_buf, b_out), (c_buf, c_out), (d_buf, d_out)))
+    ]
+    for copy in ins:
         copy.start()
-    for copy in copies:
+    for copy, onward in zip(ins, outs):
+        copy.wait()
+        onward.start()
+    for copy in outs:
         copy.wait()
 
 
@@ -367,8 +369,6 @@
         scratch_shapes=[
             pltpu.VMEM((tok, width), BF16),
             pltpu.VMEM((tok, width), F32),
-            pltpu.VMEM((tok, dh), F32),
-            pltpu.VMEM((tok, dh), F32),
             dma((4,)),
             pltpu.VMEM((reach, tok, dh), BF16),
             pltpu.VMEM((reach, tok, dh), BF16),
@@ -378,20 +378,17 @@
             pltpu.VMEM((lanes, dh), BF16),
             pltpu.VMEM((dh, lanes), BF16),
             pltpu.VMEM((dh, lanes), BF16),
+            pltpu.VMEM((reach + 1, 2, tok, dh), F32),
+            pltpu.VMEM((reach + 1, tok, dh), F32),
             pltpu.VMEM((reach, tok, dh), BF16),
             pltpu.VMEM((reach, tok, dh), BF16),
-            pltpu.VMEM((reach, tok, dh), BF16),
-            pltpu.VMEM((reach, tok, dh), BF16),
-            pltpu.VMEM((tok, dh), F32),
-            pltpu.VMEM((tok, dh), F32),
             pltpu.VMEM((2, tok, dh), F32),
-            pltpu.VMEM((heads_n - 1, 2, tok, dh), F32),
-            pltpu.VMEM((2, tok, width), BF16),
-            pltpu.VMEM((2, 2, tok, width), BF16),
-            pltpu.VMEM((2, tok, width), BF16),
-            pltpu.VMEM((2, tok, width), BF16),
-            pltpu.VMEM((8, width), F32),
-            pltpu.VMEM((8, width), F32),
+            pltpu.VMEM((2 * hh, tok, dh), BF16),
+            pltpu.VMEM((2 * hh, 2, tok, dh), BF16),
+            pltpu.VMEM((2 * hh, tok, dh), BF16),
+            pltpu.VMEM((2 * hh, tok, dh), BF16),
+            pltpu.VMEM((8, dh), F32),
+            pltpu.VMEM((8, dh), F32),
             pltpu.VMEM((tok, width), BF16),
             pltpu.VMEM((tok, dh), BF16),
             pltpu.VMEM((tok, dh), BF16),
@@ -400,11 +397,12 @@
             pltpu.SMEM((2,), jnp.int32),
             dma((6,)),
             dma((2, reach)), dma((2, reach)),
-            dma((2, reach)), dma((2, reach)),
-            dma((2, 2)), dma((2, 2)),
-            dma((2,)), dma((2,)),
+            dma((reach + 1,)), dma((reach + 1,)),
+            dma((reach,)), dma((reach,)),
+            dma((2 * hh, 2)), dma((2 * hh, 2)),
+            dma((2 * hh,)), dma((2 * hh,)),
             dma, dma,
-            dma((heads_n - 1,)), dma((heads_n - 1,)),
+            dma, dma,
         ],
         compiler_params=pltpu.CompilerParams(
             collective_id=0, has_side_effects=True, vmem_limit_bytes=VMEM_GRANT
@@ -415,7 +413,7 @@
         out_shape=results,
         in_specs=[pl.BlockSpec(memory_space=pl.ANY)] * 4,
         out_specs=(hbm,) * 4,
-        scratch_shapes=[dma((4,))],
+        scratch_shapes=[pltpu.VMEM(r.shape, r.dtype) for r in results] + [dma((4,)), dma((4,))],
         compiler_params=pltpu.CompilerParams(vmem_limit_bytes=VMEM_GRANT),
     )(*held)
 

time: 47.4 us -> 28.2 us (0.59)
  Pallas kernels: 46.6 us -> 27.4 us
    pallas_call x1, Pallas kernels: 21 us -> 1.87 us  [per_device(): pl.pallas_call(write_out, out_shape=results, in_specs=[pl.BlockSpec(memor...]
where the time goes in v3:
time: 28.2 us; the launch traced here: 28 us
  Pallas kernels  27.4 us (97%)
  between operations  0.64 us (2%)
    pallas_call x1, Pallas kernels, per_device(): pl.pallas_call(functools.partial(kernel, n, heads_n, reach, docs), out_sh...  25.5 us
    pallas_call x1, Pallas kernels, per_device(): pl.pallas_call(write_out, out_shape=results, in_specs=[pl.BlockSpec(memor...  1.87 us

profile of v3, /device:TPU:0, one launch (start us, length us, event | category | flops | bytes accessed | tf_op | source)
XLA Modules:
  0.0 28.0 jit_solution(7894128266928177118)
XLA Ops:
  0.6 25.5 %shard_map.93 = (bf16[256,256]{1,0:T(8,128)(2,1)}, f32[256,256]{1,0:T(8,128)}, f32[256,128]{1,0:T(8,128)}, f32[256,128]{1,0:T(8,128)}) custom-call(bf16[256,256]{1,0:T(8,128)(2,1)} %q_hbm.1, bf16[256,128]{1,0:T(8,128)(2,1)} %k_hbm.1, bf16[256,128]{1,0:T(8,128)(2,1)} %v_hbm.1, bf16[256,256]{1,0:T(8,128)(2,1)} %g_hbm.1, s32[16]{0:T(128)} %doc_hbm.1, s32[2]{0:T(128)} %plan_hbm.1), custom_call_target="tpu_custom_call" | custom-call | tf_op jit(solution)/shard_map/pallas_call | solution.py:364
  26.1 1.9 %shard_map.94 = (bf16[256,256]{1,0:T(8,128)(2,1)}, f32[256,256]{1,0:T(8,128)}, f32[256,128]{1,0:T(8,128)}, f32[256,128]{1,0:T(8,128)}) custom-call(bf16[256,256]{1,0:T(8,128)(2,1)} %get-tuple-element.8.a, f32[256,256]{1,0:T(8,128)} %get-tuple-element.9.b, f32[256,128]{1,0:T(8,128)} %get-tuple-element.10.c, f32[256,128]{1,0:T(8,128)} %get-tuple-element.11.d), custom_call_target="tpu_custom_call" | custom-call | tf_op jit(solution)/shard_map/pallas_call | solution.py:411

commit v4 on v3

--- a/solution.py
+++ b/solution.py
@@ -10,7 +10,7 @@
 
 HOPS = 2
 DOC_CAP = 4096
-VMEM_GRANT = 64000 * 1024
+VMEM_GRANT = 40 * 1024 * 1024
 NEG = -1e30
 MESH = pl.DeviceIdType.MESH
 F32 = jnp.float32
@@ -24,9 +24,8 @@
 def kernel(
     n, heads_n, reach, docs,
     q_hbm, k_hbm, v_hbm, g_hbm, doc_hbm, plan_hbm,
-    out_hbm, dq_hbm, dk_hbm, dv_hbm,
-    out_ref, dq_ref, store_s,
-    kbuf, vbuf, scores, wb_scr, qs, gs, qt, gt,
+    out_ref, dq_ref, dk_ref, dv_ref,
+    kbuf, vbuf, scores, wb_scr, ds_scr, gw_own, qs, gs, qt, gt,
     part, part_in, red_out, red_in, sums,
     stage, win, pick, picked, plan_own, plan_far,
     q_ref, k_ref, v_ref, g_ref, doc_ref, plan_ref, load_s,
@@ -149,7 +148,7 @@
     def values(d):
         return v_ref[...] if d == 0 else vbuf[d - 1]
 
-    top = jnp.full((1, lanes), NEG, F32)
+    tops, totals = [], []
     for d in range(reach + 1):
         if d:
 
@@ -170,25 +169,27 @@
         else:
             allowed = allowed & (t >= 0)
         raw = jnp.where(allowed, raw, NEG)
-        scores[d] = raw
-        top = jnp.maximum(top, jnp.max(raw, axis=0, keepdims=True))
-
-    total = jnp.zeros((1, lanes), F32)
+        block_top = jnp.max(raw, axis=0, keepdims=True)
+        e = jnp.exp2((raw - block_top) * factor)
+        scores[d] = e
+        tops.append(block_top)
+        totals.append(jnp.sum(e, axis=0, keepdims=True))
+        if d == 0:
+            gw_own[...] = dot(values(0), gt[...], ((1,), (0,)))
+    top = functools.reduce(jnp.maximum, tops)
+    scales = [jnp.exp2((block_top - top) * factor) for block_top in tops]
+    inverse = 1.0 / sum(total * scale for total, scale in zip(totals, scales))
+    scales = [scale * inverse for scale in scales]
+
+    att = jnp.zeros((dh, lanes), F32)
     for d in range(reach + 1):
-        e = jnp.exp2((scores[d] - top) * factor)
-        scores[d] = e
-        total = total + jnp.sum(e, axis=0, keepdims=True)
-    inverse = 1.0 / total
-
-    att = jnp.zeros((dh, lanes), F32)
-    for d in range(reach, -1, -1):
         if d:
 
             @pl.when(me >= d)
             def _():
                 v_copy(d).wait_recv()
 
-        wb = (scores[d] * inverse).astype(BF16)
+        wb = (scores[d] * scales[d]).astype(BF16)
         att = att + dot(values(d), wb, ((0,), (0,)))
         wb_scr[d] = wb
     att = att.astype(BF16)
@@ -209,14 +210,18 @@
     dots = jnp.sum(gt[...].astype(F32) * att.astype(F32), axis=0, keepdims=True)
 
     grad = jnp.zeros((dh, lanes), F32)
+    for d in range(reach + 1):
+        gw = gw_own[...] if d == 0 else dot(values(d), gt[...], ((1,), (0,)))
+        ds = (scores[d] * scales[d] * (gw - dots)).astype(BF16)
+        ds_scr[d] = ds
+        grad = grad + dot(keys(d), ds, ((0,), (0,)))
+    grad = (grad * inv_root).astype(BF16)
+    for h in range(hh):
+        send_window(hh + h, grad[:, h * tok:(h + 1) * tok].T)
+
     for d in range(reach, -1, -1):
-        value_term = dot(wb_scr[d], gs[...], ((1,), (0,)))
-        gw = dot(values(d), gt[...], ((1,), (0,)))
-        ds = (scores[d] * inverse * (gw - dots)).astype(BF16)
-        key_term = dot(ds, qs[...], ((1,), (0,))) * inv_root
-        grad = grad + dot(keys(d), ds, ((0,), (0,)))
-        part[d, 0] = key_term
-        part[d, 1] = value_term
+        part[d, 0] = dot(ds_scr[d], qs[...], ((1,), (0,))) * inv_root
+        part[d, 1] = dot(wb_scr[d], gs[...], ((1,), (0,)))
         part_copy(d).start()
     for d in range(reach, 0, -1):
         part_copy(d).wait_recv()
@@ -225,10 +230,6 @@
         @pl.when(me >= d)
         def _():
             red_copy(d).start()
-
-    grad = (grad * inv_root).astype(BF16)
-    for h in range(hh):
-        send_window(hh + h, grad[:, h * tok:(h + 1) * tok].T)
 
     plan_copy.wait_recv()
     side = lax.rem(me, 2)
@@ -265,13 +266,6 @@
             sums[my_head] += red_in[d - 1].astype(F32)
 
     sum_copy.start()
-    stores = [
-        pltpu.make_async_copy(src, dst, store_s.at[j])
-        for j, (src, dst) in enumerate((
-            (out_ref, out_hbm), (dq_ref, dq_hbm), (sums.at[0], dk_hbm), (sums.at[1], dv_hbm),
-        ))
-    ]
-
     for c in range(2 * hh):
         pick_copy(c).wait_recv()
         cols = slice((c % hh) * dh, (c % hh + 1) * dh)
@@ -289,12 +283,9 @@
                 out_ref[rows_s, cols] = acc.astype(BF16)
             else:
                 dq_ref[rows_s, cols] = acc
-        if c == hh - 1:
-            stores[0].start()
-    stores[1].start()
     sum_copy.wait_recv()
-    stores[2].start()
-    stores[3].start()
+    dk_ref[...] = sums[0]
+    dv_ref[...] = sums[1]
 
     for d in range(1, reach + 1):
 
@@ -322,25 +313,16 @@
         pick_copy(c).wait_send()
     plan_copy.wait_send()
     sum_copy.wait_send()
-    for store in stores:
-        store.wait()
-
-
-def write_out(a, b, c, d, a_out, b_out, c_out, d_out, a_buf, b_buf, c_buf, d_buf, in_sems, out_sems):
-    ins = [
-        pltpu.make_async_copy(src, dst, in_sems.at[j])
-        for j, (src, dst) in enumerate(((a, a_buf), (b, b_buf), (c, c_buf), (d, d_buf)))
+
+
+def write_out(a, b, c, d, a_out, b_out, c_out, d_out, sems):
+    copies = [
+        pltpu.make_async_copy(src, dst, sems.at[j])
+        for j, (src, dst) in enumerate(((a, a_out), (b, b_out), (c, c_out), (d, d_out)))
     ]
-    outs = [
-        pltpu.make_async_copy(src, dst, out_sems.at[j])
-        for j, (src, dst) in enumerate(((a_buf, a_out), (b_buf, b_out), (c_buf, c_out), (d_buf, d_out)))
-    ]
-    for copy in ins:
+    for copy in copies:
         copy.start()
-    for copy, onward in zip(ins, outs):
-        copy.wait()
-        onward.start()
-    for copy in outs:
+    for copy in copies:
         copy.wait()
 
 
@@ -354,6 +336,7 @@
     docs = doc_lengths.shape[0]
     lanes = hh * tok
     hbm = pl.BlockSpec(memory_space=pltpu.HBM)
+    vmem = pl.BlockSpec(memory_space=pltpu.VMEM)
     dma = pltpu.SemaphoreType.DMA
     results = (
         jax.ShapeDtypeStruct((tok, width), BF16),
@@ -363,17 +346,16 @@
     )
     held = pl.pallas_call(
         functools.partial(kernel, n, heads_n, reach, docs),
-        out_shape=results,
+        out_shape=tuple(pltpu.VMEM(r.shape, r.dtype) for r in results),
         in_specs=[hbm] * 6,
-        out_specs=(hbm,) * 4,
+        out_specs=(vmem,) * 4,
         scratch_shapes=[
-            pltpu.VMEM((tok, width), BF16),
-            pltpu.VMEM((tok, width), F32),
-            dma((4,)),
             pltpu.VMEM((reach, tok, dh), BF16),
             pltpu.VMEM((reach, tok, dh), BF16),
             pltpu.VMEM((reach + 1, tok, lanes), F32),
             pltpu.VMEM((reach + 1, tok, lanes), BF16),
+            pltpu.VMEM((reach + 1, tok, lanes), BF16),
+            pltpu.VMEM((tok, lanes), F32),
             pltpu.VMEM((lanes, dh), BF16),
             pltpu.VMEM((lanes, dh), BF16),
             pltpu.VMEM((dh, lanes), BF16),
@@ -407,13 +389,16 @@
         compiler_params=pltpu.CompilerParams(
             collective_id=0, has_side_effects=True, vmem_limit_bytes=VMEM_GRANT
         ),
-    )(queries, key_input, value_input, grad_out, doc_lengths, stretch_plan)
+    )(*(
+        pltpu.with_memory_space_constraint(arg, pltpu.HBM)
+        for arg in (queries, key_input, value_input, grad_out, doc_lengths, stretch_plan)
+    ))
     return pl.pallas_call(
         write_out,
         out_shape=results,
-        in_specs=[pl.BlockSpec(memory_space=pl.ANY)] * 4,
+        in_specs=[vmem] * 4,
         out_specs=(hbm,) * 4,
-        scratch_shapes=[pltpu.VMEM(r.shape, r.dtype) for r in results] + [dma((4,)), dma((4,))],
+        scratch_shapes=[dma((4,))],
         compiler_params=pltpu.CompilerParams(vmem_limit_bytes=VMEM_GRANT),
     )(*held)
 

time: 28.2 us -> 23.8 us (0.84)
  Pallas kernels: 27.4 us -> 23 us
    pallas_call x1, Pallas kernels: 25.5 us -> 22.2 us  [per_device(): pl.pallas_call(functools.partial(kernel, n, heads_n, reach, docs), out_sh...]
    pallas_call x1, Pallas kernels: 1.87 us -> 0.87 us  [per_device(): pl.pallas_call(write_out, out_shape=results, in_specs=[vmem] * 4, out_spe...]
where the time goes in v4:
time: 23.8 us; the launch traced here: 23.7 us
  Pallas kernels  23 us (97%)
  between operations  0.64 us (3%)
    pallas_call x1, Pallas kernels, per_device(): pl.pallas_call(functools.partial(kernel, n, heads_n, reach, docs), out_sh...  22.2 us
    pallas_call x1, Pallas kernels, per_device(): pl.pallas_call(write_out, out_shape=results, in_specs=[vmem] * 4, out_spe...  0.87 us

profile of v4, /device:TPU:0, one launch (start us, length us, event | category | flops | bytes accessed | tf_op | source)
XLA Modules:
  0.0 23.7 jit_solution(11345077935066318744)
XLA Ops:
  0.6 22.2 %shard_map.93 = (bf16[256,256]{1,0:T(8,128)(2,1)S(1)}, f32[256,256]{1,0:T(8,128)S(1)}, f32[256,128]{1,0:T(8,128)S(1)}, f32[256,128]{1,0:T(8,128)S(1)}) custom-call(bf16[256,256]{1,0:T(8,128)(2,1)} %q_hbm.1, bf16[256,128]{1,0:T(8,128)(2,1)} %k_hbm.1, bf16[256,128]{1,0:T(8,128)(2,1)} %v_hbm.1, bf16[256,256]{1,0:T(8,128)(2,1)} %g_hbm.1, s32[16]{0:T(128)} %doc_hbm.1, ...), custom_call_target="tpu_custom_call" | custom-call | tf_op jit(solution)/shard_map/pallas_call | solution.py:347
  22.8 0.9 %shard_map.94 = (bf16[256,256]{1,0:T(8,128)(2,1)}, f32[256,256]{1,0:T(8,128)}, f32[256,128]{1,0:T(8,128)}, f32[256,128]{1,0:T(8,128)}) custom-call(bf16[256,256]{1,0:T(8,128)(2,1)S(1)} %get-tuple-element.8.a, f32[256,256]{1,0:T(8,128)S(1)} %get-tuple-element.9.b, f32[256,128]{1,0:T(8,128)S(1)} %get-tuple-element.10.c, f32[256,128]{1,0:T(8,128)S(1)} %get-tuple-element.11.d), custom_call_target="tpu_custom_call" | custom-call | tf_op jit(solution)/shard_map/pallas_call | solution.py:396

commit v5 on v4

--- a/solution.py
+++ b/solution.py
@@ -29,7 +29,7 @@
     part, part_in, red_out, red_in, sums,
     stage, win, pick, picked, plan_own, plan_far,
     q_ref, k_ref, v_ref, g_ref, doc_ref, plan_ref, load_s,
-    kv_s, kv_r, part_s, part_r, red_s, red_r, win_s, win_r, pick_s, pick_r, plan_s, plan_r, sum_s, sum_r,
+    kv_s, kv_r, across_s, across_r, part_s, part_r, red_s, red_r, win_s, win_r, pick_s, pick_r, plan_s, plan_r, sum_s, sum_r,
 ):
     tok, dh = k_ref.shape
     width = q_ref.shape[1]
@@ -77,23 +77,38 @@
             device_id={"ctx": target}, device_id_type=MESH,
         )
 
-    def k_copy(d):
-        return ctx_copy(k_hbm, kbuf.at[d - 1], kv_s.at[0, d - 1], kv_r.at[0, d - 1], me + d)
-
-    def v_copy(d):
-        return ctx_copy(v_hbm, vbuf.at[d - 1], kv_s.at[1, d - 1], kv_r.at[1, d - 1], me + d)
-
     def head_copy(src, dst, s, r):
         return pltpu.make_async_remote_copy(
             src_ref=src, dst_ref=dst, send_sem=s, recv_sem=r,
             device_id={"head": 1 - my_head}, device_id_type=MESH,
         )
 
+    mine = pl.ds(pl.multiple_of(my_head * half, half), half)
+
+    def k_copy(d):
+        return ctx_copy(
+            k_hbm.at[mine], kbuf.at[d - 1, mine], kv_s.at[0, d - 1], kv_r.at[0, d - 1], me + d
+        )
+
+    def v_copy(d):
+        return ctx_copy(
+            v_hbm.at[mine], vbuf.at[d - 1, mine], kv_s.at[1, d - 1], kv_r.at[1, d - 1], me + d
+        )
+
+    def k_across(d):
+        rows = kbuf.at[d - 1, mine]
+        return head_copy(rows, rows, across_s.at[0, d - 1], across_r.at[0, d - 1])
+
+    def v_across(d):
+        rows = vbuf.at[d - 1, mine]
+        return head_copy(rows, rows, across_s.at[1, d - 1], across_r.at[1, d - 1])
+
     def part_copy(d):
         return head_copy(part.at[d, 1 - my_head], part_in.at[d], part_s.at[d], part_r.at[d])
 
     def red_copy(d):
-        return ctx_copy(red_out.at[d - 1], red_in.at[d - 1], red_s.at[d - 1], red_r.at[d - 1], me - d)
+        target = partner if d == 1 else me - d
+        return ctx_copy(red_out.at[d - 1], red_in.at[d - 1], red_s.at[d - 1], red_r.at[d - 1], target)
 
     def win_copy(c, side):
         target = me + HOPS if side == 0 else me - HOPS
@@ -150,16 +165,32 @@
 
     tops, totals = [], []
     for d in range(reach + 1):
+        if d == 1:
+            for b in range(1, reach + 1):
+
+                @pl.when(me >= b)
+                def _():
+                    k_copy(b).wait_recv()
+                    k_across(b).start()
+
+                @pl.when(me < b)
+                def _():
+                    kbuf[b - 1] = jnp.zeros((tok, dh), BF16)
+                    vbuf[b - 1] = jnp.zeros((tok, dh), BF16)
+
+        if d == reach:
+            for b in range(1, reach + 1):
+
+                @pl.when(me >= b)
+                def _():
+                    v_copy(b).wait_recv()
+                    v_across(b).start()
+
         if d:
 
             @pl.when(me >= d)
             def _():
-                k_copy(d).wait_recv()
-
-            @pl.when(me < d)
-            def _():
-                kbuf[d - 1] = jnp.zeros((tok, dh), BF16)
-                vbuf[d - 1] = jnp.zeros((tok, dh), BF16)
+                k_across(d).wait_recv()
 
         raw = dot(keys(d), qt[...], ((1,), (0,)))
         t = offset + (me - d) * tok
@@ -187,7 +218,7 @@
 
             @pl.when(me >= d)
             def _():
-                v_copy(d).wait_recv()
+                v_across(d).wait_recv()
 
         wb = (scores[d] * scales[d]).astype(BF16)
         att = att + dot(values(d), wb, ((0,), (0,)))
@@ -219,17 +250,27 @@
     for h in range(hh):
         send_window(hh + h, grad[:, h * tok:(h + 1) * tok].T)
 
-    for d in range(reach, -1, -1):
+    for d in range(1, reach + 2):
+        d = d % (reach + 1)
         part[d, 0] = dot(ds_scr[d], qs[...], ((1,), (0,))) * inv_root
         part[d, 1] = dot(wb_scr[d], gs[...], ((1,), (0,)))
         part_copy(d).start()
-    for d in range(reach, 0, -1):
+
+    odd = lax.rem(me, 2) == 1
+    for d in range(1, reach + 1):
         part_copy(d).wait_recv()
-        red_out[d - 1] = (part[d, my_head] + part_in[d]).astype(BF16)
-
-        @pl.when(me >= d)
-        def _():
+        term = part[d, my_head] + part_in[d]
+        if d == 2:
+            red_copy(1).wait_recv()
+            term = term + jnp.where(odd, red_in[0].astype(F32), 0.0)
+        red_out[d - 1] = term.astype(BF16)
+        if d == 1:
             red_copy(d).start()
+        else:
+
+            @pl.when(me >= d)
+            def _():
+                red_copy(d).start()
 
     plan_copy.wait_recv()
     side = lax.rem(me, 2)
@@ -258,7 +299,12 @@
 
     part_copy(0).wait_recv()
     sums[my_head] = part[0, my_head] + part_in[0]
-    for d in range(1, reach + 1):
+
+    @pl.when(jnp.logical_not(odd))
+    def _():
+        sums[my_head] += red_in[0].astype(F32)
+
+    for d in range(2, reach + 1):
 
         @pl.when(me + d < n)
         def _():
@@ -296,7 +342,16 @@
 
         @pl.when(me >= d)
         def _():
+            k_across(d).wait_send()
+            v_across(d).wait_send()
+
+        if d == 1:
             red_copy(d).wait_send()
+        else:
+
+            @pl.when(me >= d)
+            def _():
+                red_copy(d).wait_send()
 
     for d in range(reach + 1):
         part_copy(d).wait_send()
@@ -379,6 +434,7 @@
             pltpu.SMEM((2,), jnp.int32),
             dma((6,)),
             dma((2, reach)), dma((2, reach)),
+            dma((2, reach)), dma((2, reach)),
             dma((reach + 1,)), dma((reach + 1,)),
             dma((reach,)), dma((reach,)),
             dma((2 * hh, 2)), dma((2 * hh, 2)),

time: 23.8 us -> 23.6 us (level)
  the two profiles are of different devices: /device:TPU:0 before, /device:TPU:8 now
where the time goes in v5:
time: 23.6 us; the launch traced here: 23.5 us
  Pallas kernels  22.8 us (97%)
  between operations  0.64 us (3%)
    pallas_call x1, Pallas kernels, per_device(): pl.pallas_call(functools.partial(kernel, n, heads_n, reach, docs), out_sh...  22 us
    pallas_call x1, Pallas kernels, per_device(): pl.pallas_call(write_out, out_shape=results, in_specs=[vmem] * 4, out_spe...  0.87 us

profile of v5, /device:TPU:8, one launch (start us, length us, event | category | flops | bytes accessed | tf_op | source)
XLA Modules:
  0.0 23.5 jit_solution(7108415427158340928)
XLA Ops:
  0.6 22.0 %shard_map.93 = (bf16[256,256]{1,0:T(8,128)(2,1)S(1)}, f32[256,256]{1,0:T(8,128)S(1)}, f32[256,128]{1,0:T(8,128)S(1)}, f32[256,128]{1,0:T(8,128)S(1)}) custom-call(bf16[256,256]{1,0:T(8,128)(2,1)} %q_hbm.1, bf16[256,128]{1,0:T(8,128)(2,1)} %k_hbm.1, bf16[256,128]{1,0:T(8,128)(2,1)} %v_hbm.1, bf16[256,256]{1,0:T(8,128)(2,1)} %g_hbm.1, s32[16]{0:T(128)} %doc_hbm.1, ...), custom_call_target="tpu_custom_call" | custom-call | tf_op jit(solution)/shard_map/pallas_call | solution.py:402
  22.6 0.9 %shard_map.94 = (bf16[256,256]{1,0:T(8,128)(2,1)}, f32[256,256]{1,0:T(8,128)}, f32[256,128]{1,0:T(8,128)}, f32[256,128]{1,0:T(8,128)}) custom-call(bf16[256,256]{1,0:T(8,128)(2,1)S(1)} %get-tuple-element.8.a, f32[256,256]{1,0:T(8,128)S(1)} %get-tuple-element.9.b, f32[256,128]{1,0:T(8,128)S(1)} %get-tuple-element.10.c, f32[256,128]{1,0:T(8,128)S(1)} %get-tuple-element.11.d), custom_call_target="tpu_custom_call" | custom-call | tf_op jit(solution)/shard_map/pallas_call | solution.py:452

commit v6 on v4

--- a/solution.py
+++ b/solution.py
@@ -77,23 +77,24 @@
             device_id={"ctx": target}, device_id_type=MESH,
         )
 
-    def k_copy(d):
-        return ctx_copy(k_hbm, kbuf.at[d - 1], kv_s.at[0, d - 1], kv_r.at[0, d - 1], me + d)
-
-    def v_copy(d):
-        return ctx_copy(v_hbm, vbuf.at[d - 1], kv_s.at[1, d - 1], kv_r.at[1, d - 1], me + d)
-
     def head_copy(src, dst, s, r):
         return pltpu.make_async_remote_copy(
             src_ref=src, dst_ref=dst, send_sem=s, recv_sem=r,
             device_id={"head": 1 - my_head}, device_id_type=MESH,
         )
 
+    def k_copy(d):
+        return ctx_copy(k_hbm, kbuf.at[d - 1], kv_s.at[0, d - 1], kv_r.at[0, d - 1], me + d)
+
+    def v_copy(d):
+        return ctx_copy(v_hbm, vbuf.at[d - 1], kv_s.at[1, d - 1], kv_r.at[1, d - 1], me + d)
+
     def part_copy(d):
         return head_copy(part.at[d, 1 - my_head], part_in.at[d], part_s.at[d], part_r.at[d])
 
     def red_copy(d):
-        return ctx_copy(red_out.at[d - 1], red_in.at[d - 1], red_s.at[d - 1], red_r.at[d - 1], me - d)
+        target = partner if d == 1 else me - d
+        return ctx_copy(red_out.at[d - 1], red_in.at[d - 1], red_s.at[d - 1], red_r.at[d - 1], target)
 
     def win_copy(c, side):
         target = me + HOPS if side == 0 else me - HOPS
@@ -219,22 +220,16 @@
     for h in range(hh):
         send_window(hh + h, grad[:, h * tok:(h + 1) * tok].T)
 
-    for d in range(reach, -1, -1):
+    for d in range(1, reach + 2):
+        d = d % (reach + 1)
         part[d, 0] = dot(ds_scr[d], qs[...], ((1,), (0,))) * inv_root
         part[d, 1] = dot(wb_scr[d], gs[...], ((1,), (0,)))
         part_copy(d).start()
-    for d in range(reach, 0, -1):
-        part_copy(d).wait_recv()
-        red_out[d - 1] = (part[d, my_head] + part_in[d]).astype(BF16)
-
-        @pl.when(me >= d)
-        def _():
-            red_copy(d).start()
 
     plan_copy.wait_recv()
     side = lax.rem(me, 2)
     other = me + HOPS - 2 * HOPS * side
-    for c in range(2 * hh):
+    def send_pick(c):
 
         @pl.when(me >= HOPS)
         def _():
@@ -256,9 +251,35 @@
             pick[c, s * half:(s + 1) * half, :] = acc.astype(BF16)
         pick_copy(c).start()
 
+    odd = lax.rem(me, 2) == 1
+    for d in range(1, reach + 1):
+        part_copy(d).wait_recv()
+        term = part[d, my_head] + part_in[d]
+        if d == 2:
+            red_copy(1).wait_recv()
+            term = term + jnp.where(odd, red_in[0].astype(F32), 0.0)
+        red_out[d - 1] = term.astype(BF16)
+        if d == 1:
+            red_copy(d).start()
+            for c in range(hh):
+                send_pick(c)
+        else:
+
+            @pl.when(me >= d)
+            def _():
+                red_copy(d).start()
+
+    for c in range(hh, 2 * hh):
+        send_pick(c)
+
     part_copy(0).wait_recv()
     sums[my_head] = part[0, my_head] + part_in[0]
-    for d in range(1, reach + 1):
+
+    @pl.when(jnp.logical_not(odd))
+    def _():
+        sums[my_head] += red_in[0].astype(F32)
+
+    for d in range(2, reach + 1):
 
         @pl.when(me + d < n)
         def _():
@@ -294,9 +315,13 @@
             k_copy(d).wait_send()
             v_copy(d).wait_send()
 
-        @pl.when(me >= d)
-        def _():
+        if d == 1:
             red_copy(d).wait_send()
+        else:
+
+            @pl.when(me >= d)
+            def _():
+                red_copy(d).wait_send()
 
     for d in range(reach + 1):
         part_copy(d).wait_send()

time: 23.8 us -> 24.3 us (1.021)
  Pallas kernels: 23 us -> 23.5 us
    pallas_call x1, Pallas kernels: 22.2 us -> 22.6 us  [per_device(): pl.pallas_call(functools.partial(kernel, n, heads_n, reach, docs), out_sh...]
where the time goes in v6:
time: 24.3 us; the launch traced here: 24.1 us
  Pallas kernels  23.5 us (97%)
  between operations  0.64 us (3%)
    pallas_call x1, Pallas kernels, per_device(): pl.pallas_call(functools.partial(kernel, n, heads_n, reach, docs), out_sh...  22.6 us
    pallas_call x1, Pallas kernels, per_device(): pl.pallas_call(write_out, out_shape=results, in_specs=[vmem] * 4, out_spe...  0.87 us

profile of v6, /device:TPU:0, one launch (start us, length us, event | category | flops | bytes accessed | tf_op | source)
XLA Modules:
  0.0 24.1 jit_solution(18129476140854552030)
XLA Ops:
  0.6 22.6 %shard_map.93 = (bf16[256,256]{1,0:T(8,128)(2,1)S(1)}, f32[256,256]{1,0:T(8,128)S(1)}, f32[256,128]{1,0:T(8,128)S(1)}, f32[256,128]{1,0:T(8,128)S(1)}) custom-call(bf16[256,256]{1,0:T(8,128)(2,1)} %q_hbm.1, bf16[256,128]{1,0:T(8,128)(2,1)} %k_hbm.1, bf16[256,128]{1,0:T(8,128)(2,1)} %v_hbm.1, bf16[256,256]{1,0:T(8,128)(2,1)} %g_hbm.1, s32[16]{0:T(128)} %doc_hbm.1, ...), custom_call_target="tpu_custom_call" | custom-call | tf_op jit(solution)/shard_map/pallas_call | solution.py:372
  23.3 0.9 %shard_map.94 = (bf16[256,256]{1,0:T(8,128)(2,1)}, f32[256,256]{1,0:T(8,128)}, f32[256,128]{1,0:T(8,128)}, f32[256,128]{1,0:T(8,128)}) custom-call(bf16[256,256]{1,0:T(8,128)(2,1)S(1)} %get-tuple-element.8.a, f32[256,256]{1,0:T(8,128)S(1)} %get-tuple-element.9.b, f32[256,128]{1,0:T(8,128)S(1)} %get-tuple-element.10.c, f32[256,128]{1,0:T(8,128)S(1)} %get-tuple-element.11.d), custom_call_target="tpu_custom_call" | custom-call | tf_op jit(solution)/shard_map/pallas_call | solution.py:421

commit v7 on v5

--- a/solution.py
+++ b/solution.py
@@ -107,8 +107,7 @@
         return head_copy(part.at[d, 1 - my_head], part_in.at[d], part_s.at[d], part_r.at[d])
 
     def red_copy(d):
-        target = partner if d == 1 else me - d
-        return ctx_copy(red_out.at[d - 1], red_in.at[d - 1], red_s.at[d - 1], red_r.at[d - 1], target)
+        return ctx_copy(red_out.at[d - 1], red_in.at[d - 1], red_s.at[d - 1], red_r.at[d - 1], me - d)
 
     def win_copy(c, side):
         target = me + HOPS if side == 0 else me - HOPS
@@ -250,27 +249,17 @@
     for h in range(hh):
         send_window(hh + h, grad[:, h * tok:(h + 1) * tok].T)
 
-    for d in range(1, reach + 2):
-        d = d % (reach + 1)
+    for d in range(reach, -1, -1):
         part[d, 0] = dot(ds_scr[d], qs[...], ((1,), (0,))) * inv_root
         part[d, 1] = dot(wb_scr[d], gs[...], ((1,), (0,)))
         part_copy(d).start()
-
-    odd = lax.rem(me, 2) == 1
-    for d in range(1, reach + 1):
+    for d in range(reach, 0, -1):
         part_copy(d).wait_recv()
-        term = part[d, my_head] + part_in[d]
-        if d == 2:
-            red_copy(1).wait_recv()
-            term = term + jnp.where(odd, red_in[0].astype(F32), 0.0)
-        red_out[d - 1] = term.astype(BF16)
-        if d == 1:
+        red_out[d - 1] = (part[d, my_head] + part_in[d]).astype(BF16)
+
+        @pl.when(me >= d)
+        def _():
             red_copy(d).start()
-        else:
-
-            @pl.when(me >= d)
-            def _():
-                red_copy(d).start()
 
     plan_copy.wait_recv()
     side = lax.rem(me, 2)
@@ -300,11 +289,7 @@
     part_copy(0).wait_recv()
     sums[my_head] = part[0, my_head] + part_in[0]
 
-    @pl.when(jnp.logical_not(odd))
-    def _():
-        sums[my_head] += red_in[0].astype(F32)
-
-    for d in range(2, reach + 1):
+    for d in range(1, reach + 1):
 
         @pl.when(me + d < n)
         def _():
@@ -345,13 +330,9 @@
             k_across(d).wait_send()
             v_across(d).wait_send()
 
-        if d == 1:
+        @pl.when(me >= d)
+        def _():
             red_copy(d).wait_send()
-        else:
-
-            @pl.when(me >= d)
-            def _():
-                red_copy(d).wait_send()
 
     for d in range(reach + 1):
         part_copy(d).wait_send()

time: 23.6 us -> 23.1 us (0.979)
  the two profiles are of different devices: /device:TPU:8 before, /device:TPU:0 now
where the time goes in v7:
time: 23.1 us; the launch traced here: 23 us
  Pallas kernels  22.3 us (97%)
  between operations  0.64 us (3%)
    pallas_call x1, Pallas kernels, per_device(): pl.pallas_call(functools.partial(kernel, n, heads_n, reach, docs), out_sh...  21.5 us
    pallas_call x1, Pallas kernels, per_device(): pl.pallas_call(write_out, out_shape=results, in_specs=[vmem] * 4, out_spe...  0.87 us

profile of v7, /device:TPU:0, one launch (start us, length us, event | category | flops | bytes accessed | tf_op | source)
XLA Modules:
  0.0 23.0 jit_solution(1747064431606058740)
XLA Ops:
  0.6 21.5 %shard_map.93 = (bf16[256,256]{1,0:T(8,128)(2,1)S(1)}, f32[256,256]{1,0:T(8,128)S(1)}, f32[256,128]{1,0:T(8,128)S(1)}, f32[256,128]{1,0:T(8,128)S(1)}) custom-call(bf16[256,256]{1,0:T(8,128)(2,1)} %q_hbm.1, bf16[256,128]{1,0:T(8,128)(2,1)} %k_hbm.1, bf16[256,128]{1,0:T(8,128)(2,1)} %v_hbm.1, bf16[256,256]{1,0:T(8,128)(2,1)} %g_hbm.1, s32[16]{0:T(128)} %doc_hbm.1, ...), custom_call_target="tpu_custom_call" | custom-call | tf_op jit(solution)/shard_map/pallas_call | solution.py:383
  22.1 0.9 %shard_map.94 = (bf16[256,256]{1,0:T(8,128)(2,1)}, f32[256,256]{1,0:T(8,128)}, f32[256,128]{1,0:T(8,128)}, f32[256,128]{1,0:T(8,128)}) custom-call(bf16[256,256]{1,0:T(8,128)(2,1)S(1)} %get-tuple-element.8.a, f32[256,256]{1,0:T(8,128)S(1)} %get-tuple-element.9.b, f32[256,128]{1,0:T(8,128)S(1)} %get-tuple-element.10.c, f32[256,128]{1,0:T(8,128)S(1)} %get-tuple-element.11.d), custom_call_target="tpu_custom_call" | custom-call | tf_op jit(solution)/shard_map/pallas_call | solution.py:433

commit v8 on v7

--- a/solution.py
+++ b/solution.py
@@ -211,7 +211,6 @@
     inverse = 1.0 / sum(total * scale for total, scale in zip(totals, scales))
     scales = [scale * inverse for scale in scales]
 
-    att = jnp.zeros((dh, lanes), F32)
     for d in range(reach + 1):
         if d:
 
@@ -220,10 +219,7 @@
                 v_across(d).wait_recv()
 
         wb = (scores[d] * scales[d]).astype(BF16)
-        att = att + dot(values(d), wb, ((0,), (0,)))
         wb_scr[d] = wb
-    att = att.astype(BF16)
-
     def send_window(c, rows):
         stage[c] = rows
 
@@ -235,8 +231,13 @@
         def _():
             win_copy(c, 1).start()
 
+    heads = []
     for h in range(hh):
-        send_window(h, att[:, h * tok:(h + 1) * tok].T)
+        cols = slice(h * tok, (h + 1) * tok)
+        terms = [dot(values(d), wb_scr[d, :, cols], ((0,), (0,))) for d in range(reach + 1)]
+        heads.append(sum(terms).astype(BF16))
+        send_window(h, heads[h].T)
+    att = jnp.concatenate(heads, axis=1)
     dots = jnp.sum(gt[...].astype(F32) * att.astype(F32), axis=0, keepdims=True)
 
     grad = jnp.zeros((dh, lanes), F32)

time: 23.1 us -> 23.1 us (level)
  no operation moved by 1% of the time
where the time goes in v8:
time: 23.1 us; the launch traced here: 22.9 us
  Pallas kernels  22.3 us (97%)
  between operations  0.64 us (3%)
    pallas_call x1, Pallas kernels, per_device(): pl.pallas_call(functools.partial(kernel, n, heads_n, reach, docs), out_sh...  21.4 us
    pallas_call x1, Pallas kernels, per_device(): pl.pallas_call(write_out, out_shape=results, in_specs=[vmem] * 4, out_spe...  0.87 us

profile of v8, /device:TPU:0, one launch (start us, length us, event | category | flops | bytes accessed | tf_op | source)
XLA Modules:
  0.0 22.9 jit_solution(12651948378906305457)
XLA Ops:
  0.6 21.4 %shard_map.93 = (bf16[256,256]{1,0:T(8,128)(2,1)S(1)}, f32[256,256]{1,0:T(8,128)S(1)}, f32[256,128]{1,0:T(8,128)S(1)}, f32[256,128]{1,0:T(8,128)S(1)}) custom-call(bf16[256,256]{1,0:T(8,128)(2,1)} %q_hbm.1, bf16[256,128]{1,0:T(8,128)(2,1)} %k_hbm.1, bf16[256,128]{1,0:T(8,128)(2,1)} %v_hbm.1, bf16[256,256]{1,0:T(8,128)(2,1)} %g_hbm.1, s32[16]{0:T(128)} %doc_hbm.1, ...), custom_call_target="tpu_custom_call" | custom-call | tf_op jit(solution)/shard_map/pallas_call | solution.py:384
  22.1 0.9 %shard_map.94 = (bf16[256,256]{1,0:T(8,128)(2,1)}, f32[256,256]{1,0:T(8,128)}, f32[256,128]{1,0:T(8,128)}, f32[256,128]{1,0:T(8,128)}) custom-call(bf16[256,256]{1,0:T(8,128)(2,1)S(1)} %get-tuple-element.8.a, f32[256,256]{1,0:T(8,128)S(1)} %get-tuple-element.9.b, f32[256,128]{1,0:T(8,128)S(1)} %get-tuple-element.10.c, f32[256,128]{1,0:T(8,128)S(1)} %get-tuple-element.11.d), custom_call_target="tpu_custom_call" | custom-call | tf_op jit(solution)/shard_map/pallas_call | solution.py:434
